TPU v7x, 128 devices: a whole 4x4x4 slice. The times are simulated.
128 devices in a mesh: gx: 8 (over y, core), gy: 16 (over z, x).
Axes of the slice: x: 4, y: 4, z: 4, core: 2. Of those that a mesh axis runs over, the one named last changes fastest.
Arguments:
- fields: float32 [5, 8, 2048, 2048], P(None, None, 'gx', 'gy'), may hold values from -8 to 8
Outputs:
- x_derivative: float32 [5, 8, 2048, 2048], P(None, None, 'gx', 'gy')
- y_derivative: float32 [5, 8, 2048, 2048], P(None, None, 'gx', 'gy')
- smoothed: float32 [5, 8, 2048, 2048], P(None, None, 'gx', 'gy')
All inputs are finite; a program needn't handle non-finite values.
Results may differ from a plain program's by a relative error of at most 0.0003.
Values sent between devices are 32-bit elements; how exact they have to be, the bound alone decides.
No kernel may reach another device: no remote copies, remote signals or barrier semaphores. Data moves between devices by JAX's collectives and lax.ppermute only.
A program may use at most 192 MiB of HBM per device.

v0:
```python
import math

import jax
import jax.numpy as jnp
import numpy as np
from jax import lax
from jax.sharding import PartitionSpec as P

deriv_offdiag = 1.0 / 3.0
coef_near = 14.0 / 9.0
coef_far = 1.0 / 9.0
filter_offdiag = 0.45
rim_width = 5
inner_span_count = 48


def padded_2(cells, sides, width):
    for axis, dim in sides:
        count = lax.axis_size(axis)
        head = lax.slice_in_dim(cells, 0, width, axis=dim)
        tail = lax.slice_in_dim(cells, cells.shape[dim] - width, cells.shape[dim], axis=dim)
        cells = jnp.concatenate(
            [
                lax.ppermute(tail, axis, [(i, (i + 1) % count) for i in range(count)]),
                cells,
                lax.ppermute(head, axis, [((i + 1) % count, i) for i in range(count)]),
            ],
            axis=dim,
        )
    return cells


def filter_weights():
    return [
        (193.0 + 126.0 * filter_offdiag) / 256.0,
        (105.0 + 302.0 * filter_offdiag) / 256.0,
        15.0 * (2.0 * filter_offdiag - 1.0) / 64.0,
        45.0 * (1.0 - 2.0 * filter_offdiag) / 512.0,
        5.0 * (2.0 * filter_offdiag - 1.0) / 256.0,
        (1.0 - 2.0 * filter_offdiag) / 512.0,
    ]


def stencil_rows():
    weights = filter_weights()
    deriv_taps = [
        (-2, -coef_far / 4.0),
        (-1, -coef_near / 2.0),
        (1, coef_near / 2.0),
        (2, coef_far / 4.0),
    ]
    smoothing_coefficients = [(0, weights[0])]
    for tap_order in range(1, 6):
        smoothing_coefficients.append((tap_order, weights[tap_order] / 2.0))
        smoothing_coefficients.append((-tap_order, weights[tap_order] / 2.0))
    return ((deriv_offdiag, deriv_taps), (filter_offdiag, smoothing_coefficients))


def line_tables(cell_count, rim_cells):
    row_ids = np.arange(cell_count)
    operators = []
    lowers = []
    uppers = []
    corners = []
    for adjacent_band_entry, tap_list in stencil_rows():
        banded = np.zeros((cell_count, cell_count + 2 * rim_cells))
        spread = rim_cells - rim_width
        squared_term_gap = math.sqrt(1.0 - 4.0 * adjacent_band_entry * adjacent_band_entry)
        attenuation_ratio = (squared_term_gap - 1.0) / (2.0 * adjacent_band_entry)
        for offset, weight in tap_list:
            for distance_count in range(-spread, spread + 1):
                green_function_value = attenuation_ratio ** abs(distance_count) / squared_term_gap
                banded[row_ids, row_ids + rim_cells + offset + distance_count] += (
                    weight * green_function_value
                )
        operators.append(banded)
        lowers.append(np.zeros(cell_count))
        uppers.append(np.zeros(cell_count))
        corners.append(0.0)
    return (
        jnp.asarray(np.array(operators), jnp.float32),
        jnp.asarray(np.array(lowers), jnp.float32),
        jnp.asarray(np.array(uppers), jnp.float32),
        jnp.asarray(np.array(corners), jnp.float32),
    )


def on_device(fields):
    cells_x = fields.shape[2]
    cells_y = fields.shape[3]
    padded = padded_2(fields, (("gx", 2), ("gy", 3)), inner_span_count)
    x_input = padded[:, :, :, inner_span_count:-inner_span_count]
    y_input = padded[:, :, inner_span_count:-inner_span_count, :]
    operators_x, lowers_x, uppers_x, corners_x = line_tables(cells_x, inner_span_count)
    answer_along_first = jnp.einsum(
        "oij,fzjy->ofziy", operators_x, x_input, precision=lax.Precision.HIGHEST
    )
    x_derivative = answer_along_first[0]
    filtered_wide = padded_2(answer_along_first[1], (("gy", 3),), inner_span_count)
    operators_y, lowers_y, uppers_y, corners_y = line_tables(cells_y, inner_span_count)
    deriv_part = jnp.einsum(
        "ij,fzxj->fzxi", operators_y[0], y_input, precision=lax.Precision.HIGHEST
    )
    lowpass_portion = jnp.einsum(
        "ij,fzxj->fzxi", operators_y[1], filtered_wide, precision=lax.Precision.HIGHEST
    )
    solved_y = jnp.stack([deriv_part, lowpass_portion], axis=0)
    return (x_derivative, solved_y[0], solved_y[1])


def solution(mesh):
    placed = (P(None, None, "gx", "gy"),)
    return jax.shard_map(
        on_device,
        mesh=mesh,
        in_specs=placed,
        out_specs=(P(None, None, "gx", "gy"), P(None, None, "gx", "gy"), P(None, None, "gx", "gy")),
        check_vma=False,
    )
```

profile of v0, /device:TPU:0, one launch (start us, length us, event | category | flops | bytes accessed | tf_op | source)
XLA Modules:
  0.0 233.7 jit_solution(10791862391451964899)
XLA Ops:
  0.6 1.8 fusion.17
  2.5 0.0 collective-permute-start
  2.5 2.9 %collective-permute-start.1 = (f32[5,8,48,128]{3,2,1,0:T(8,128)S(1)}, f32[5,8,48,128]{3,2,1,0:T(8,128)S(1)}, u32[]{:S(2)}, u32[]{:S(2)}) collective-permute-start(f32[5,8,48,128]{3,2,1,0:T(8,128)S(1)} %get-tuple-element.15), channel_id=1, source_target_pairs={{16,0},{32,16},{48,32},{64,48},{80,64},{96,80},{112,96},{0,112},{1... | collective-permute-start | bytes 2949128 | tf_op jit(solution)/shard_map/ppermute | solution.py:26
  5.4 11.8 %collective-permute-done = f32[5,8,48,128]{3,2,1,0:T(8,128)S(1)} collective-permute-done((f32[5,8,48,128]{3,2,1,0:T(8,128)S(1)}, f32[5,8,48,128]{3,2,1,0:T(8,128)S(1)}, u32[]{:S(2)}, u32[]{:S(2)}) %collective-permute-start) | collective-permute-done | bytes 983072 | tf_op jit(solution)/shard_map/ppermute | solution.py:24
  17.2 1.1 constant_dynamic-update-slice_fusion.2
  18.3 2.9 %constant_dynamic-update-slice_fusion.1 = f32[5,8,352,128]{3,2,1,0:T(8,128)} fusion(f32[5,8,352,128]{3,2,1,0:T(8,128)} %constant_dynamic-update-slice_fusion.2, f32[5,8,256,128]{3,2,1,0:T(8,128)S(1)} %copy-done), kind=kLoop, calls=%fused_computation.16 | loop fusion | bytes 10485760
  21.2 0.0 collective-permute-done.1
  21.2 1.1 constant_dynamic-update-slice_fusion
  22.3 12.3 %fusion.15 = (f32[5,8,352,48]{3,2,1,0:T(8,128)}, f32[5,8,352,48]{3,2,1,0:T(8,128)}) fusion(f32[5,8,352,128]{3,2,1,0:T(8,128)} %constant_dynamic-update-slice_fusion), kind=kLoop, calls=%fused_computation.20 | loop fusion | bytes 10813440 | tf_op jit(solution)/shard_map/slice | solution.py:21
  34.6 18.8 %fusion.10 = f32[2,5,8,256,128]{3,4,0,2,1:T(8,128)S(1)} fusion(f32[2,256,352,1,1]{1,2,0,4,3:T(8,128)S(1)} %copy-done.1, f32[5,8,352,128]{3,2,1,0:T(8,128)} %constant_dynamic-update-slice_fusion), kind=kOutput, calls=%fused_computation.14 | convolution fusion | flops 11072962560 | bytes 18415616 | tf_op jit(solution)/shard_map/oij,fzjy->ofziy/dot_general | solution.py:95
  53.4 4.9 %slice_bitcast_fusion = (f32[5,8,256,128]{2,3,1,0:T(8,128)}, f32[5,8,256,128]{2,3,1,0:T(8,128)}) fusion(f32[2,5,8,256,128]{3,4,0,2,1:T(8,128)S(1)} %fusion.10), kind=kLoop, calls=%fused_computation.12 | loop fusion | bytes 20971520 | tf_op jit(solution)/shard_map/squeeze | solution.py:99
  58.3 6.1 %copy.8 = f32[5,8,352,48]{2,3,1,0:T(8,128)} copy(f32[5,8,352,48]{3,2,1,0:T(8,128)} %get-tuple-element.11) | data formatting | bytes 5406720 | tf_op jit(solution)/shard_map/slice | solution.py:21
  64.4 4.8 %copy.9 = f32[5,8,352,48]{2,3,1,0:T(8,128)S(1)} copy(f32[5,8,352,48]{3,2,1,0:T(8,128)} %get-tuple-element.12) | data formatting | bytes 5406720 | tf_op jit(solution)/shard_map/slice | solution.py:20
  69.2 6.4 %collective-permute-start.3 = (f32[5,8,352,48]{2,3,1,0:T(8,128)S(1)}, f32[5,8,352,48]{2,3,1,0:T(8,128)}, u32[]{:S(2)}, u32[]{:S(2)}) collective-permute-start(f32[5,8,352,48]{2,3,1,0:T(8,128)S(1)} %copy.9), channel_id=1, source_target_pairs={{1,0},{2,1},{3,2},{4,3},{5,4},{6,5},{7,6},{8,7},{9,8},{10,9},{11,1... | collective-permute-start | bytes 8110088 | tf_op jit(solution)/shard_map/ppermute | solution.py:26
  75.6 0.0 collective-permute-start.2
  75.6 4.4 %fusion.16 = (f32[5,8,256,48]{2,3,1,0:T(8,128)}, f32[5,8,256,48]{2,3,1,0:T(8,128)}) fusion(f32[5,8,256,128]{2,3,1,0:T(8,128)} %get-tuple-element.9), kind=kLoop, calls=%fused_computation.21 | loop fusion | bytes 7864320 | tf_op jit(solution)/shard_map/slice | solution.py:21
  80.0 5.3 %collective-permute-start.5 = (f32[5,8,256,48]{2,3,1,0:T(8,128)}, f32[5,8,256,48]{2,3,1,0:T(8,128)}, u32[]{:S(2)}, u32[]{:S(2)}) collective-permute-start(f32[5,8,256,48]{2,3,1,0:T(8,128)} %get-tuple-element.14), channel_id=1, source_target_pairs={{1,0},{2,1},{3,2},{4,3},{5,4},{6,5},{7,6},{8,7},{9,8},{10,9},{11,1... | collective-permute-start | bytes 5898248 | tf_op jit(solution)/shard_map/ppermute | solution.py:26
  85.4 5.9 %copy.13 = f32[5,8,256,128]{3,2,1,0:T(8,128)} copy(f32[5,8,256,128]{2,3,1,0:T(8,128)} %get-tuple-element.10) | data formatting | bytes 10485760
  91.3 93.6 %collective-permute-done.4 = f32[5,8,256,48]{2,3,1,0:T(8,128)} collective-permute-done((f32[5,8,256,48]{2,3,1,0:T(8,128)}, f32[5,8,256,48]{2,3,1,0:T(8,128)}, u32[]{:S(2)}, u32[]{:S(2)}) %collective-permute-start.4) | collective-permute-done | bytes 1966112 | tf_op jit(solution)/shard_map/ppermute | solution.py:24
  184.9 20.5 %fusion.2 = f32[5,8,256,128]{3,2,1,0:T(8,128)} fusion(f32[128,224,1,1]{0,1,3,2:T(8,128)S(1)} %copy-done.3, f32[5,8,256,48]{2,3,1,0:T(8,128)} %collective-permute-done.5, f32[5,8,256,128]{2,3,1,0:T(8,128)} %get-tuple-element.9, f32[5,8,256,48]{2,3,1,0:T(8,128)} %collective-permute-done.4), kind=kOutput, calls=%fused_computation.4 | convolution fusion | flops 3527802880 | bytes 14532608 | tf_op jit(solution)/shard_map/ij,fzxj->fzxi/dot_general | solution.py:104
  205.4 0.0 collective-permute-done.2
  205.4 6.1 %copy.10 = f32[5,8,352,48]{3,2,1,0:T(8,128)} copy(f32[5,8,352,48]{2,3,1,0:T(8,128)} %collective-permute-done.2) | data formatting | bytes 5406720 | tf_op jit(solution)/shard_map/ppermute | solution.py:24
  211.5 6.1 %copy.11 = f32[5,8,352,48]{3,2,1,0:T(8,128)} copy(f32[5,8,352,48]{2,3,1,0:T(8,128)} %collective-permute-done.3) | data formatting | bytes 5406720 | tf_op jit(solution)/shard_map/ppermute | solution.py:26
  217.6 16.1 %fusion = f32[5,8,256,128]{3,2,1,0:T(8,128)} fusion(f32[128,224,1,1]{0,1,3,2:T(8,128)S(1)} %copy-done.2, f32[5,8,352,48]{3,2,1,0:T(8,128)} %copy.11, f32[5,8,352,128]{3,2,1,0:T(8,128)} %constant_dynamic-update-slice_fusion, f32[5,8,352,48]{3,2,1,0:T(8,128)} %copy.10), kind=kOutput, calls=%fused_computation.1 | convolution fusion | flops 3527802880 | bytes 17973248 | tf_op jit(solution)/shard_map/ij,fzxj->fzxi/dot_general | solution.py:101
  (11 shorter events, 0.0 us)
Async XLA Ops:
  0.6 17.7 %copy-start = (f32[5,8,256,128]{3,2,1,0:T(8,128)S(1)}, f32[5,8,256,128]{3,2,1,0:T(8,128)}, u32[]{:S(2)}) copy-start(f32[5,8,256,128]{3,2,1,0:T(8,128)} %param.3) | copy-start | bytes 15728644
  2.5 14.7 %collective-permute-start = (f32[5,8,48,128]{3,2,1,0:T(8,128)S(1)}, f32[5,8,48,128]{3,2,1,0:T(8,128)S(1)}, u32[]{:S(2)}, u32[]{:S(2)}) collective-permute-start(f32[5,8,48,128]{3,2,1,0:T(8,128)S(1)} %get-tuple-element.16), channel_id=1, source_target_pairs={{0,16},{16,32},{32,48},{48,64},{64,80},{80,96},{96,112},{112,0},{1... | collective-permute-start | bytes 2949128 | tf_op jit(solution)/shard_map/ppermute | solution.py:24
  2.5 18.8 %collective-permute-start.1 = (f32[5,8,48,128]{3,2,1,0:T(8,128)S(1)}, f32[5,8,48,128]{3,2,1,0:T(8,128)S(1)}, u32[]{:S(2)}, u32[]{:S(2)}) collective-permute-start(f32[5,8,48,128]{3,2,1,0:T(8,128)S(1)} %get-tuple-element.15), channel_id=1, source_target_pairs={{16,0},{32,16},{48,32},{64,48},{80,64},{96,80},{112,96},{0,112},{1... | collective-permute-start | bytes 2949128 | tf_op jit(solution)/shard_map/ppermute | solution.py:26
  22.3 12.3 %copy-start.1 = (f32[2,256,352,1,1]{1,2,0,4,3:T(8,128)S(1)}, f32[2,256,352,1,1]{1,2,0,4,3:T(8,128)}, u32[]{:S(2)}) copy-start(f32[2,256,352,1,1]{1,2,0,4,3:T(8,128)} %constant.10) | copy-start | bytes 2162692
  69.2 142.3 %collective-permute-start.3 = (f32[5,8,352,48]{2,3,1,0:T(8,128)S(1)}, f32[5,8,352,48]{2,3,1,0:T(8,128)}, u32[]{:S(2)}, u32[]{:S(2)}) collective-permute-start(f32[5,8,352,48]{2,3,1,0:T(8,128)S(1)} %copy.9), channel_id=1, source_target_pairs={{1,0},{2,1},{3,2},{4,3},{5,4},{6,5},{7,6},{8,7},{9,8},{10,9},{11,1... | collective-permute-start | bytes 8110088 | tf_op jit(solution)/shard_map/ppermute | solution.py:26
  75.6 129.8 %collective-permute-start.2 = (f32[5,8,352,48]{2,3,1,0:T(8,128)}, f32[5,8,352,48]{2,3,1,0:T(8,128)}, u32[]{:S(2)}, u32[]{:S(2)}) collective-permute-start(f32[5,8,352,48]{2,3,1,0:T(8,128)} %copy.8), channel_id=1, source_target_pairs={{0,1},{1,2},{2,3},{3,4},{4,5},{5,6},{6,7},{7,8},{8,9},{9,10},{10,1... | collective-permute-start | bytes 8110088 | tf_op jit(solution)/shard_map/ppermute | solution.py:24
  80.0 104.8 %copy-start.3 = (f32[128,224,1,1]{0,1,3,2:T(8,128)S(1)}, f32[128,224,1,1]{0,1,3,2:T(8,128)}, u32[]{:S(2)}) copy-start(f32[128,224,1,1]{0,1,3,2:T(8,128)} %constant.12) | copy-start | bytes 344068
  80.0 104.8 %collective-permute-start.4 = (f32[5,8,256,48]{2,3,1,0:T(8,128)}, f32[5,8,256,48]{2,3,1,0:T(8,128)}, u32[]{:S(2)}, u32[]{:S(2)}) collective-permute-start(f32[5,8,256,48]{2,3,1,0:T(8,128)} %get-tuple-element.13), channel_id=1, source_target_pairs={{0,1},{1,2},{2,3},{3,4},{4,5},{5,6},{6,7},{7,8},{8,9},{9,10},{10,1... | collective-permute-start | bytes 5898248 | tf_op jit(solution)/shard_map/ppermute | solution.py:24
  80.0 104.8 %collective-permute-start.5 = (f32[5,8,256,48]{2,3,1,0:T(8,128)}, f32[5,8,256,48]{2,3,1,0:T(8,128)}, u32[]{:S(2)}, u32[]{:S(2)}) collective-permute-start(f32[5,8,256,48]{2,3,1,0:T(8,128)} %get-tuple-element.14), channel_id=1, source_target_pairs={{1,0},{2,1},{3,2},{4,3},{5,4},{6,5},{7,6},{8,7},{9,8},{10,9},{11,1... | collective-permute-start | bytes 5898248 | tf_op jit(solution)/shard_map/ppermute | solution.py:26
  211.5 6.1 %copy-start.2 = (f32[128,224,1,1]{0,1,3,2:T(8,128)S(1)}, f32[128,224,1,1]{0,1,3,2:T(8,128)}, u32[]{:S(2)}) copy-start(f32[128,224,1,1]{0,1,3,2:T(8,128)} %constant.11) | copy-start | bytes 344068
where the time goes:
time: 234 us
  waiting for transfers between devices  105 us (45%)
  local copies, waits for them, and re-layouts  57.5 us (25%)
  matrix products  55.4 us (24%)
  starting transfers between devices  14.7 us (6%)
    ppermute x3, waiting for transfers between devices, padded_2(): lax.ppermute(tail, axis, [(i, (i + 1) % count) for i in range(count)])  105 us
    slice x3, local copies, waits for them, and re-layouts, padded_2(): lax.slice_in_dim(cells, cells.shape[dim] - width, cells.shape[dim], axis=...  22.9 us
    dot_general x1, matrix products, on_device(): jnp.einsum('ij,fzxj->fzxi', operators_y[1], filtered_wide, precision=lax....  20.5 us
    dot_general x1, matrix products, on_device(): jnp.einsum('oij,fzjy->ofziy', operators_x, x_input, precision=lax.Precisi...  18.8 us
    dot_general x1, matrix products, on_device(): jnp.einsum('ij,fzxj->fzxi', operators_y[0], y_input, precision=lax.Precis...  16.1 us
    ppermute x3, starting transfers between devices, padded_2(): lax.ppermute(head, axis, [((i + 1) % count, i) for i in range(count)])  14.7 us
    unnamed x11, local copies, waits for them, and re-layouts  9.93 us
    slice x2, local copies, waits for them, and re-layouts, padded_2(): head = lax.slice_in_dim(cells, 0, width, axis=dim)  6.57 us
  transfers between devices with their start and end apart: 6, of which 2 were waited for; matrix products, arithmetic and copies ran while one was open for 18% of the time, Pallas kernels for 0%

commit v1 on v0

v1 whole, which is shorter than its diff:
```python
import math

import jax
import jax.numpy as jnp
import ml_dtypes
import numpy as np
from jax import lax
from jax.experimental import pallas as pl
from jax.experimental.pallas import tpu as pltpu
from jax.sharding import PartitionSpec as P

F32 = jnp.float32
BF16 = jnp.bfloat16
deriv_offdiag = 1.0 / 3.0
coef_near = 14.0 / 9.0
coef_far = 1.0 / 9.0
filter_offdiag = 0.45
reach = 64
filter_rim = 48
deriv_rim = 24
group = 8


def filter_weights():
    return [
        (193.0 + 126.0 * filter_offdiag) / 256.0,
        (105.0 + 302.0 * filter_offdiag) / 256.0,
        15.0 * (2.0 * filter_offdiag - 1.0) / 64.0,
        45.0 * (1.0 - 2.0 * filter_offdiag) / 512.0,
        5.0 * (2.0 * filter_offdiag - 1.0) / 256.0,
        (1.0 - 2.0 * filter_offdiag) / 512.0,
    ]


class Line:
    def __init__(self, offdiag, taps, sign, width):
        gap = math.sqrt(1.0 - 4.0 * offdiag * offdiag)
        self.ratio = (gap - 1.0) / (2.0 * offdiag)
        self.gap = gap
        self.taps = taps
        self.sign = sign
        far = width + 4
        self.scale = self.tap(far) / self.ratio**far
        self.near = [0.0] + [
            self.tap(n) - self.scale * self.ratio**n if n <= width else 0.0 for n in range(1, 2 * far)
        ]

    def tap(self, n):
        return sum(w * self.ratio ** abs(n - o) / self.gap for o, w in self.taps)

    def block(self, cells):
        values = np.array([self.tap(n) for n in range(-cells + 1, cells)])
        ids = np.arange(cells)
        return values[ids[None, :] - ids[:, None] + cells - 1]

    def near_at(self, n):
        return self.near[n] if 0 < n < len(self.near) else 0.0

    def from_below(self, cells):
        table = np.zeros((cells, 5))
        for i in range(cells):
            table[i, 0] = self.sign * self.scale * self.ratio ** (i + 1)
            for k in range(4):
                table[i, 1 + k] = self.sign * self.near_at(i + 4 - k)
        return table

    def from_above(self, cells):
        table = np.zeros((cells, 5))
        for i in range(cells):
            table[i, 0] = self.scale * self.ratio ** (cells - i)
            for k in range(4):
                table[i, 1 + k] = self.near_at(cells + k - i)
        return table


def line_operators():
    weights = filter_weights()
    deriv_taps = [
        (-2, -coef_far / 4.0),
        (-1, -coef_near / 2.0),
        (1, coef_near / 2.0),
        (2, coef_far / 4.0),
    ]
    filter_taps = [(0, weights[0])]
    for order in range(1, 6):
        filter_taps.append((order, weights[order] / 2.0))
        filter_taps.append((-order, weights[order] / 2.0))
    return Line(deriv_offdiag, deriv_taps, -1.0, 1), Line(filter_offdiag, filter_taps, 1.0, 4)


def halves(table):
    hi = np.asarray(table, np.float32).astype(ml_dtypes.bfloat16)
    lo = (np.asarray(table, np.float64) - hi.astype(np.float64)).astype(ml_dtypes.bfloat16)
    return hi, lo


def split(values):
    hi = values.astype(BF16)
    return hi, (values - hi.astype(F32)).astype(BF16)


def dot(a, b, dims=((1,), (0,))):
    return lax.dot_general(a, b, (dims, ((), ())), preferred_element_type=F32)


def lanes(column):
    return np.repeat(np.asarray(column, np.float32)[:, None], 128, axis=1)


VMEM = pl.BlockSpec(memory_space=pltpu.VMEM)
ANY = pl.BlockSpec(memory_space=pl.ANY)


def call(name, kernel, outs, ins, flops, nbytes, out_specs=None, scratch=(), limit=20):
    return pl.pallas_call(
        kernel,
        in_specs=[VMEM] * len(ins),
        out_specs=out_specs or [VMEM] * len(outs),
        out_shape=[jax.ShapeDtypeStruct(shape, F32) for shape in outs],
        scratch_shapes=list(scratch),
        compiler_params=pltpu.CompilerParams(vmem_limit_bytes=limit << 20),
        cost_estimate=pl.CostEstimate(flops=flops, bytes_accessed=nbytes, transcendentals=0),
        name=name,
    )(*ins)


def face_kernel(f, wf_head, wd_head, wf_tail, wd_tail, ty, x_down, x_up, y_down, y_up):
    planes, rows, _ = f.shape
    short = wd_head.shape[0]

    def step(i, carry):
        for j in range(group):
            p = i * group + j
            head = f[p, :reach, :]
            tail = f[p, rows - reach :, :]
            row = pl.ds(p, 1)
            x_down[0, row, :] = jnp.sum(head * wf_head[...], axis=0, keepdims=True)
            x_up[0, row, :] = jnp.sum(tail * wf_tail[...], axis=0, keepdims=True)
            x_down[5, row, :] = jnp.sum(head[:short] * wd_head[...], axis=0, keepdims=True)
            x_up[5, row, :] = jnp.sum(tail[reach - short :] * wd_tail[...], axis=0, keepdims=True)
            for k in range(4):
                x_down[1 + k, row, :] = f[p, k : k + 1, :]
                x_up[1 + k, row, :] = f[p, rows - 4 + k : rows - 3 + k, :]
            both = jnp.concatenate(split(f[p]), axis=-1)
            r = dot(ty[...], both, ((1,), (1,)))
            r = r[:16] + r[16:]
            for k in range(6):
                y_down[k, row, :] = r[k : k + 1]
                y_up[k, row, :] = r[8 + k : 9 + k]
        return carry

    lax.fori_loop(0, planes // group, step, 0)


def x_product(f, w, i):
    hi, lo = split(jnp.concatenate([f[2 * i], f[2 * i + 1]], axis=-1))
    n = hi.shape[0]
    return dot(w[:, :n], hi) + dot(w[:, n:], hi) + dot(w[:, :n], lo)


def filter_x_kernel(f, w, out):
    planes = f.shape[0]
    pairs = group // 2

    def step(i, carry):
        for j in range(pairs):
            q = i * pairs + j
            r = x_product(f, w, q)
            out[2 * q] = r[:, :128]
            out[2 * q + 1] = r[:, 128:]
        return carry

    lax.fori_loop(0, planes // group, step, 0)


def corner_kernel(lower, upper, ty_hi, ty_lo, out):
    planes = lower.shape[1]
    rows = jnp.concatenate([lower[k] for k in range(5)] + [upper[k] for k in range(5)], axis=0)
    hi, lo = split(rows)
    r = dot(hi, ty_hi[...]) + dot(hi, ty_lo[...]) + dot(lo, ty_hi[...])
    total = r[:planes]
    for k in range(1, 10):
        total = total + pltpu.roll(r[k * planes : (k + 1) * planes], 10 * k, 1)
    out[...] = total


def add_rims(values, low, high):
    n = low.shape[0]
    return jnp.concatenate([values[:n] + low, values[n:-n], values[-n:] + high], axis=0)


def filter_rims(lower, upper, s_low, s_high, c_low, c_high, row):
    low = s_low[...] * lower[0, row, :]
    high = s_high[...] * upper[0, row, :]
    near_low = c_low[0] * lower[1, row, :]
    near_high = c_high[0] * upper[1, row, :]
    for k in range(1, 4):
        near_low = near_low + c_low[k] * lower[1 + k, row, :]
        near_high = near_high + c_high[k] * upper[1 + k, row, :]
    low = jnp.concatenate([low[:8] + near_low, low[8:]], axis=0)
    high = jnp.concatenate([high[:-8], high[-8:] + near_high], axis=0)
    return low, high


def deriv_rims(lower, upper, s_low, s_high, c_low, c_high, row):
    low = s_low[...] * lower[5, row, :]
    high = s_high[...] * upper[5, row, :]
    low = jnp.concatenate([low[:8] + c_low[...] * lower[4, row, :], low[8:]], axis=0)
    high = jnp.concatenate([high[:-8], high[-8:] + c_high[...] * upper[1, row, :]], axis=0)
    return low, high


def middle_kernel(
    f, fx, lower, upper, wx, wy_d, wy_f, fs_low, fs_high, fc_low, fc_high, ds_low, ds_high, dc_low, dc_high,
    dx_out, dy, sm, dx, sems,
):
    planes = f.shape[0]
    pairs = group // 2

    def x_step(i, carry):
        for j in range(pairs):
            q = i * pairs + j
            r = x_product(f, wx, q)
            for half in range(2):
                p = 2 * q + half
                low, high = deriv_rims(lower, upper, ds_low, ds_high, dc_low, dc_high, pl.ds(p, 1))
                dx[p] = add_rims(r[:, 128 * half : 128 * half + 128], low, high)
        part = pl.ds(i * group, group)
        pltpu.make_async_copy(dx.at[part], dx_out.at[part], sems.at[i]).start()
        return carry

    lax.fori_loop(0, planes // group, x_step, 0)

    def y_step(i, carry):
        for j in range(group):
            p = i * group + j
            r = dot(jnp.concatenate(split(f[p]), axis=-1), wy_d[...])
            dy[p] = r[:, :128] + r[:, 128:]
            low, high = filter_rims(lower, upper, fs_low, fs_high, fc_low, fc_high, pl.ds(p, 1))
            r = dot(jnp.concatenate(split(add_rims(fx[p], low, high)), axis=-1), wy_f[...])
            sm[p] = r[:, :128] + r[:, 128:]
        return carry

    lax.fori_loop(0, planes // group, y_step, 0)
    for i in range(planes // group):
        part = pl.ds(i * group, group)
        pltpu.make_async_copy(dx.at[part], dx_out.at[part], sems.at[i]).wait()


def last_kernel(
    dy, sm, lower, upper, z_lower, z_upper, ax, ux, v, dy_out, sm_out, halo, dy_full, sm_full, sems
):
    planes = dy.shape[0]
    n = ax.shape[0]
    rows = jnp.concatenate([lower[k] for k in range(5)] + [upper[k] for k in range(5)], axis=0)
    hi, lo = split(rows)
    filtered = dot(hi, ax[:, :n]) + dot(hi, ax[:, n:]) + dot(lo, ax[:, :n])
    corners = jnp.concatenate(
        [pltpu.roll(z_lower[...], 128 - 5 - g, 1) for g in range(5)]
        + [z_upper[...]]
        + [pltpu.roll(z_upper[...], 128 - g, 1) for g in range(1, 5)],
        axis=0,
    )
    hi, lo = split(corners)
    filtered = filtered + dot(hi, ux[:, :n]) + dot(hi, ux[:, n:]) + dot(lo, ux[:, :n])
    zero = jnp.zeros((planes, n), F32)
    table = [filtered[k * planes : (k + 1) * planes] for k in range(5)] + [lower[5], lower[4], zero]
    table += [filtered[(5 + k) * planes : (6 + k) * planes] for k in range(5)] + [upper[5], upper[1], zero]
    for k in range(16):
        for c in range(0, n, 128):
            halo[c // 128, pl.ds(k, planes, stride=16), :] = table[k][:, c : c + 128]

    def step(i, carry):
        for j in range(group):
            p = i * group + j
            at = pl.ds(pl.multiple_of(p * 16, 16), 16)
            hi, lo = split(jnp.concatenate([halo[c, at, :] for c in range(n // 128)], axis=-1))
            r = dot(jnp.concatenate([hi, lo, hi], axis=0), v[...], ((0,), (0,)))
            dy_full[p] = dy[p] + r[:, :128]
            sm_full[p] = sm[p] + r[:, 128:]
        part = pl.ds(i * group, group)
        pltpu.make_async_copy(dy_full.at[part], dy_out.at[part], sems.at[0, i]).start()
        pltpu.make_async_copy(sm_full.at[part], sm_out.at[part], sems.at[1, i]).start()
        return carry

    lax.fori_loop(0, planes // group, step, 0)
    for i in range(planes // group):
        part = pl.ds(i * group, group)
        pltpu.make_async_copy(dy_full.at[part], dy_out.at[part], sems.at[0, i]).wait()
        pltpu.make_async_copy(sm_full.at[part], sm_out.at[part], sems.at[1, i]).wait()


def tables(rows, cols):
    deriv, smooth = line_operators()
    t = {}
    for name, line in (("d", deriv), ("f", smooth)):
        hi, lo = halves(line.block(rows))
        t["wx_" + name] = np.concatenate([hi, lo], axis=1)
        hi, lo = halves(line.block(cols).T)
        t["wy_" + name] = np.block([[hi, lo], [hi, np.zeros_like(lo)]])
    hi, lo = halves(smooth.block(rows).T)
    t["ax"] = np.concatenate([hi, lo], axis=1)
    powers = lambda line, count: line.ratio ** np.arange(count)
    short = 32
    t["wf_head"] = lanes(powers(smooth, reach))
    t["wf_tail"] = lanes(powers(smooth, reach)[::-1])
    t["wd_head"] = lanes(powers(deriv, short))
    t["wd_tail"] = lanes(powers(deriv, short)[::-1])
    ty = np.zeros((16, cols))
    ty[0] = powers(smooth, cols)
    ty[8] = ty[0][::-1]
    for k in range(4):
        ty[1 + k, k] = 1.0
        ty[9 + k, cols - 4 + k] = 1.0
    ty[5] = powers(deriv, cols)
    ty[13] = ty[5][::-1]
    hi, lo = halves(ty)
    t["ty"] = np.block([[hi, hi], [lo, np.zeros_like(lo)]])
    columns = np.zeros((cols, 128))
    columns[:, :5] = ty[:5].T
    columns[:, 5:10] = ty[8:13].T
    t["ty_hi"], t["ty_lo"] = halves(columns)
    low, high = smooth.from_below(rows), smooth.from_above(rows)
    ux = np.zeros((128, rows))
    for k in range(5):
        ux[10 * k] = low[:, k]
        ux[10 * (5 + k)] = high[:, k]
    hi, lo = halves(ux)
    t["ux"] = np.concatenate([hi, lo], axis=1)
    t["fs_low"], t["fs_high"] = lanes(low[:filter_rim, 0]), lanes(high[-filter_rim:, 0])
    t["fc_low"] = np.stack([lanes(low[:8, 1 + k]) for k in range(4)])
    t["fc_high"] = np.stack([lanes(high[-8:, 1 + k]) for k in range(4)])
    low, high = deriv.from_below(rows), deriv.from_above(rows)
    t["ds_low"], t["ds_high"] = lanes(low[:deriv_rim, 0]), lanes(high[-deriv_rim:, 0])
    t["dc_low"], t["dc_high"] = lanes(low[:8, 4]), lanes(high[-8:, 1])
    v = np.zeros((16, 2 * cols))
    low, high = smooth.from_below(cols), smooth.from_above(cols)
    v[0:5, cols:], v[8:13, cols:] = low.T, high.T
    low, high = deriv.from_below(cols), deriv.from_above(cols)
    v[5, :cols], v[6, :cols] = low[:, 0], low[:, 4]
    v[13, :cols], v[14, :cols] = high[:, 0], high[:, 1]
    hi, lo = halves(v)
    t["v"] = np.concatenate([hi, hi, lo], axis=0)
    return {key: jnp.asarray(value) for key, value in t.items()}


def shifted(values, axis, by):
    count = lax.axis_size(axis)
    return lax.ppermute(values, axis, [(i, (i + by) % count) for i in range(count)])


def on_device(fields):
    shape = fields.shape
    rows, cols = shape[2:]
    planes = shape[0] * shape[1]
    block = (planes, rows, cols)
    f = fields.reshape(block)
    t = tables(rows, cols)
    x_face, y_face = (6, planes, cols), (6, planes, rows)
    x_down, x_up, y_down, y_up = call(
        "faces", face_kernel, [x_face, x_face, y_face, y_face],
        [f] + [t[k] for k in ("wf_head", "wd_head", "wf_tail", "wd_tail", "ty")], 10**9, 10**7,
    )
    y_lower = shifted(y_up, "gy", 1)
    y_upper = shifted(y_down, "gy", -1)
    x_lower = shifted(x_up, "gx", 1)
    x_upper = shifted(x_down, "gx", -1)
    (fx,) = call("filter_x", filter_x_kernel, [block], [f, t["wx_f"]], 2 * 10**9, 10**7)
    (corner,) = call(
        "corners", corner_kernel, [(planes, 128)], [x_lower, x_upper, t["ty_hi"], t["ty_lo"]], 10**8, 10**6
    )
    z_lower = shifted(corner, "gy", 1)
    z_upper = shifted(corner, "gy", -1)
    rims = ("fs_low", "fs_high", "fc_low", "fc_high", "ds_low", "ds_high", "dc_low", "dc_high")
    dx, dy, sm = call(
        "middle", middle_kernel, [block, block, block],
        [f, fx, x_lower, x_upper] + [t[k] for k in ("wx_d", "wy_d", "wy_f") + rims], 6 * 10**9, 2 * 10**7,
        out_specs=[ANY, VMEM, VMEM],
        scratch=[pltpu.VMEM(block, F32), pltpu.SemaphoreType.DMA((planes // group,))],
    )
    dy, sm = call(
        "last", last_kernel, [block, block],
        [dy, sm, y_lower, y_upper, z_lower, z_upper, t["ax"], t["ux"], t["v"]], 10**9, 2 * 10**7,
        out_specs=[ANY, ANY],
        scratch=[
            pltpu.VMEM((rows // 128, planes * 16, 128), F32),
            pltpu.VMEM(block, F32),
            pltpu.VMEM(block, F32),
            pltpu.SemaphoreType.DMA((2, planes // group)),
        ],
        limit=24,
    )
    return tuple(out.reshape(shape) for out in (dx, dy, sm))


def solution(mesh):
    placed = P(None, None, "gx", "gy")
    return jax.shard_map(
        on_device, mesh=mesh, in_specs=(placed,), out_specs=(placed, placed, placed), check_vma=False
    )
```

time: 234 us -> 36.8 us (0.16)
  waiting for transfers between devices: 105 us -> 0.35 us
  matrix products: 55.4 us -> 0 us
  local copies, waits for them, and re-layouts: 57.5 us -> 6.25 us
  Pallas kernels: 0 us -> 17.4 us
  starting transfers between devices: 14.7 us -> 11.5 us
    ppermute x6, waiting for transfers between devices: 105 us -> 0.35 us  [shifted(): lax.ppermute(values, axis, [(i, (i + by) % count) for i in range(count)])]
    dot_general x3 -> x0, matrix products: 55.4 us -> none  [the longest x1 20.5 us: on_device(): jnp.einsum('ij,fzxj->fzxi', operators_y[1], filtered_wide, precision=lax....]
    slice x5 -> x0, local copies, waits for them, and re-layouts: 29.4 us -> none  [the longest x3 22.9 us: padded_2(): lax.slice_in_dim(cells, cells.shape[dim] - width, cells.shape[dim], axis=...]
    pallas_call x0 -> x5, Pallas kernels: none -> 17.4 us  [call(): pl.pallas_call(kernel, in_specs=[VMEM] * len(ins), out_specs=out_specs or...]
    ppermute x2 -> x0, local copies, waits for them, and re-layouts: 12.2 us -> none  [the longest x1 6.11 us: padded_2(): lax.ppermute(head, axis, [((i + 1) % count, i) for i in range(count)])]
    squeeze x1 -> x0, local copies, waits for them, and re-layouts: 4.87 us -> none  [on_device(): answer_along_first[1]]
    unnamed x11 -> x48, local copies, waits for them, and re-layouts: 9.93 us -> 6.25 us
    ppermute x6, starting transfers between devices: 14.7 us -> 11.5 us  [shifted(): lax.ppermute(values, axis, [(i, (i + by) % count) for i in range(count)])]
  transfers between devices with their start and end apart: 6 -> 6, of which waited for: 2 -> 1; matrix products, arithmetic and copies ran while one was open for 18% -> 0% of each run, Pallas kernels for 0% -> 27%
where the time goes in v1:
time: 36.8 us; the launch traced here: 36.4 us
  Pallas kernels  17.4 us (47%)
  starting transfers between devices  11.5 us (31%)
  local copies, waits for them, and re-layouts  6.25 us (17%)
  between operations  0.93 us (3%)
    pallas_call x5, Pallas kernels, call(): pl.pallas_call(kernel, in_specs=[VMEM] * len(ins), out_specs=out_specs or...  17.4 us
    ppermute x6, starting transfers between devices, shifted(): lax.ppermute(values, axis, [(i, (i + by) % count) for i in range(count)])  11.5 us
    unnamed x48, local copies, waits for them, and re-layouts  6.25 us
  transfers between devices with their start and end apart: 6, of which 1 were waited for; matrix products, arithmetic and copies ran while one was open for 0% of the time, Pallas kernels for 27%

profile of v1, /device:TPU:0, one launch (start us, length us, event | category | flops | bytes accessed | tf_op | source)
XLA Modules:
  0.0 36.4 jit_solution(315898893588588584)
XLA Ops:
  0.6 2.5 %copy-done = f32[5,8,256,128]{3,2,1,0:T(8,128)S(1)} copy-done((f32[5,8,256,128]{3,2,1,0:T(8,128)S(1)}, f32[5,8,256,128]{3,2,1,0:T(8,128)}, u32[]{:S(2)}) %copy-start) | copy-done | bytes 5242904
  3.1 0.8 %copy-done.3 = f32[64,128]{1,0:T(8,128)S(1)} copy-done((f32[64,128]{1,0:T(8,128)S(1)}, f32[64,128]{1,0:T(8,128)}, u32[]{:S(2)}) %copy-start.3) | copy-done | bytes 32792
  3.9 0.8 %copy-done.4 = f32[64,128]{1,0:T(8,128)S(1)} copy-done((f32[64,128]{1,0:T(8,128)S(1)}, f32[64,128]{1,0:T(8,128)}, u32[]{:S(2)}) %copy-start.4) | copy-done | bytes 32792
  4.6 0.7 %copy-done.6 = bf16[32,256]{1,0:T(8,128)(2,1)S(1)} copy-done((bf16[32,256]{1,0:T(8,128)(2,1)S(1)}, bf16[32,256]{1,0:T(8,128)(2,1)}, u32[]{:S(2)}) %copy-start.6) | copy-done | bytes 16408
  5.4 0.7 %copy-done.7 = f32[32,128]{1,0:T(8,128)S(1)} copy-done((f32[32,128]{1,0:T(8,128)S(1)}, f32[32,128]{1,0:T(8,128)}, u32[]{:S(2)}) %copy-start.7) | copy-done | bytes 16408
  6.1 0.7 %copy-done.8 = f32[32,128]{1,0:T(8,128)S(1)} copy-done((f32[32,128]{1,0:T(8,128)S(1)}, f32[32,128]{1,0:T(8,128)}, u32[]{:S(2)}) %copy-start.8) | copy-done | bytes 16408
  6.8 2.3 %faces.1 = (f32[6,40,128]{2,1,0:T(8,128)S(1)}, f32[6,40,128]{2,1,0:T(8,128)S(1)}, f32[6,40,256]{2,1,0:T(8,128)S(1)}, f32[6,40,256]{2,1,0:T(8,128)S(1)}) custom-call(f32[40,256,128]{2,1,0:T(8,128)S(1)} %bitcast.4, f32[64,128]{1,0:T(8,128)S(1)} %copy-done.4, f32[32,128]{1,0:T(8,128)S(1)} %copy-done.8, f32[64,128]{1,0:T(8,128)S(1)} %copy-done.3, ...), custom_call_target="tpu_custom_call" | custom-call | flops 1000000000 | bytes 10000000 | tf_op jit(solution)/shard_map/faces/pallas_call | solution.py:115
  9.1 0.0 collective-permute-start
  9.1 2.9 %collective-permute-start.1 = (f32[6,40,128]{2,1,0:T(8,128)S(1)}, f32[6,40,128]{2,1,0:T(8,128)S(1)}, u32[]{:S(2)}, u32[]{:S(2)}) collective-permute-start(f32[6,40,128]{2,1,0:T(8,128)S(1)} %get-tuple-element.13), channel_id=1, source_target_pairs={{0,112},{16,0},{32,16},{48,32},{64,48},{80,64},{96,80},{112,96},{1... | collective-permute-start | bytes 368648 | tf_op jit(solution)/shard_map/ppermute | solution.py:349
  12.0 1.6 %collective-permute-start.2 = (f32[6,40,256]{2,1,0:T(8,128)S(1)}, f32[6,40,256]{2,1,0:T(8,128)S(1)}, u32[]{:S(2)}, u32[]{:S(2)}) collective-permute-start(f32[6,40,256]{2,1,0:T(8,128)S(1)} %get-tuple-element.17), channel_id=1, source_target_pairs={{0,1},{1,2},{2,3},{3,4},{4,5},{5,6},{6,7},{7,8},{8,9},{9,10},{10,1... | collective-permute-start | bytes 737288 | tf_op jit(solution)/shard_map/ppermute | solution.py:349
  13.6 0.0 copy-start.9
  13.6 0.0 copy-start.10
  13.7 0.0 copy-start.11
  13.7 0.0 copy-start.15
  13.7 0.0 copy-start.16
  13.7 0.0 copy-start.17
  13.8 4.8 %collective-permute-start.3 = (f32[6,40,256]{2,1,0:T(8,128)S(1)}, f32[6,40,256]{2,1,0:T(8,128)S(1)}, u32[]{:S(2)}, u32[]{:S(2)}) collective-permute-start(f32[6,40,256]{2,1,0:T(8,128)S(1)} %get-tuple-element.18), channel_id=1, source_target_pairs={{0,15},{1,0},{2,1},{3,2},{4,3},{5,4},{6,5},{7,6},{8,7},{9,8},{10,9... | collective-permute-start | bytes 737288 | tf_op jit(solution)/shard_map/ppermute | solution.py:349
  18.6 2.9 %filter_x.1.fx = f32[40,256,128]{2,1,0:T(8,128)S(1)} custom-call(f32[40,256,128]{2,1,0:T(8,128)S(1)} %bitcast.5, bf16[256,512]{1,0:T(8,128)(2,1)S(1)} %copy-done.1), custom_call_target="tpu_custom_call" | custom-call | flops 2000000000 | bytes 10000000 | tf_op jit(solution)/shard_map/filter_x/pallas_call | solution.py:115
  21.6 0.4 %corners.1 = f32[40,128]{1,0:T(8,128)S(1)} custom-call(f32[6,40,128]{2,1,0:T(8,128)S(1)} %collective-permute-done.lower, f32[6,40,128]{2,1,0:T(8,128)S(1)} %collective-permute-done.1.upper, bf16[128,128]{1,0:T(8,128)(2,1)S(1)} %copy-done.13, bf16[128,128]{1,0:T(8,128)(2,1)S(1)} %copy-done.12), custom_call_target="tpu_custom_call" | custom-call | flops 100000000 | bytes 1000000 | tf_op jit(solution)/shard_map/corners/pallas_call | solution.py:115
  22.0 2.1 %collective-permute-start.5 = (f32[40,128]{1,0:T(8,128)S(1)}, f32[40,128]{1,0:T(8,128)S(1)}, u32[]{:S(2)}, u32[]{:S(2)}) collective-permute-start(f32[40,128]{1,0:T(8,128)S(1)} %corners.1), channel_id=1, source_target_pairs={{0,15},{1,0},{2,1},{3,2},{4,3},{5,4},{6,5},{7,6},{8,7},{9,8},{10,9... | collective-permute-start | bytes 61448 | tf_op jit(solution)/shard_map/ppermute | solution.py:349
  24.1 0.0 collective-permute-start.4
  24.2 6.6 %middle.1 = (f32[40,256,128]{2,1,0:T(8,128)}, f32[40,256,128]{2,1,0:T(8,128)S(1)}, f32[40,256,128]{2,1,0:T(8,128)S(1)}) custom-call(f32[40,256,128]{2,1,0:T(8,128)S(1)} %bitcast.8, f32[40,256,128]{2,1,0:T(8,128)S(1)} %filter_x.1.fx, f32[6,40,128]{2,1,0:T(8,128)S(1)} %collective-permute-done.lower, f32[6,40,128]{2,1,0:T(8,128)S(1)} %collective-permute-done.1.upper, ...), custom_call_target="tpu_custom_call" | custom-call | flops 6000000000 | bytes 20000000 | tf_op jit(solution)/shard_map/middle/pallas_call | solution.py:115
  30.8 0.3 collective-permute-done.4.z_lower
  31.2 5.2 %last.1 = (f32[40,256,128]{2,1,0:T(8,128)}, f32[40,256,128]{2,1,0:T(8,128)}) custom-call(f32[40,256,128]{2,1,0:T(8,128)S(1)} %get-tuple-element.15.dy, f32[40,256,128]{2,1,0:T(8,128)S(1)} %get-tuple-element.16.sm, f32[6,40,256]{2,1,0:T(8,128)S(1)} %collective-permute-done.2.lower, f32[6,40,256]{2,1,0:T(8,128)S(1)} %collective-permute-done.3.upper, ...), custom_call_target="tpu_custom_call" | custom-call | flops 1000000000 | bytes 20000000 | tf_op jit(solution)/shard_map/last/pallas_call | solution.py:115
  (42 shorter events, 0.1 us)
Async XLA Ops:
  6.8 11.8 %copy-start.1 = (bf16[256,512]{1,0:T(8,128)(2,1)S(1)}, bf16[256,512]{1,0:T(8,128)(2,1)}, u32[]{:S(2)}) copy-start(bf16[256,512]{1,0:T(8,128)(2,1)} %constant.44.clone.w.ax) | copy-start | bytes 786436
  9.1 12.5 %collective-permute-start = (f32[6,40,128]{2,1,0:T(8,128)S(1)}, f32[6,40,128]{2,1,0:T(8,128)S(1)}, u32[]{:S(2)}, u32[]{:S(2)}) collective-permute-start(f32[6,40,128]{2,1,0:T(8,128)S(1)} %get-tuple-element.12), channel_id=1, source_target_pairs={{0,16},{16,32},{32,48},{48,64},{64,80},{80,96},{96,112},{112,0},{1... | collective-permute-start | bytes 368648 | tf_op jit(solution)/shard_map/ppermute | solution.py:349
  9.1 12.4 %collective-permute-start.1 = (f32[6,40,128]{2,1,0:T(8,128)S(1)}, f32[6,40,128]{2,1,0:T(8,128)S(1)}, u32[]{:S(2)}, u32[]{:S(2)}) collective-permute-start(f32[6,40,128]{2,1,0:T(8,128)S(1)} %get-tuple-element.13), channel_id=1, source_target_pairs={{0,112},{16,0},{32,16},{48,32},{64,48},{80,64},{96,80},{112,96},{1... | collective-permute-start | bytes 368648 | tf_op jit(solution)/shard_map/ppermute | solution.py:349
  12.0 19.1 %collective-permute-start.2 = (f32[6,40,256]{2,1,0:T(8,128)S(1)}, f32[6,40,256]{2,1,0:T(8,128)S(1)}, u32[]{:S(2)}, u32[]{:S(2)}) collective-permute-start(f32[6,40,256]{2,1,0:T(8,128)S(1)} %get-tuple-element.17), channel_id=1, source_target_pairs={{0,1},{1,2},{2,3},{3,4},{4,5},{5,6},{6,7},{7,8},{8,9},{9,10},{10,1... | collective-permute-start | bytes 737288 | tf_op jit(solution)/shard_map/ppermute | solution.py:349
  13.6 10.5 %slice-start = ((s8[5242880]{0:T(1024)(128)(4,1)}), s8[4194304]{0:T(1024)(128)(4,1)S(1)}, s32[]{:S(2)}) async-start(s8[5242880]{0:T(1024)(128)(4,1)} %bitcast.6), calls=%async_computation | async-start | bytes 8388608
  13.6 7.9 %copy-start.12 = (bf16[128,128]{1,0:T(8,128)(2,1)S(1)}, bf16[128,128]{1,0:T(8,128)(2,1)}, u32[]{:S(2)}) copy-start(bf16[128,128]{1,0:T(8,128)(2,1)} %constant.52.clone.ty_lo) | copy-start | bytes 98308
  13.6 7.9 %copy-start.13 = (bf16[128,128]{1,0:T(8,128)(2,1)S(1)}, bf16[128,128]{1,0:T(8,128)(2,1)}, u32[]{:S(2)}) copy-start(bf16[128,128]{1,0:T(8,128)(2,1)} %constant.51.clone.ty_hi) | copy-start | bytes 98308
  13.6 10.4 %slice-start.1 = ((s8[5242880]{0:T(1024)(128)(4,1)}), s8[1048576]{0:T(1024)(128)(4,1)S(1)}, s32[]{:S(2)}) async-start(s8[5242880]{0:T(1024)(128)(4,1)} %bitcast.6), calls=%async_computation.1 | async-start | bytes 2097152
  13.6 10.4 %copy-start.9 = (bf16[256,512]{1,0:T(8,128)(2,1)S(1)}, bf16[256,512]{1,0:T(8,128)(2,1)}, u32[]{:S(2)}) copy-start(bf16[256,512]{1,0:T(8,128)(2,1)} %constant.42.clone.wx) | copy-start | bytes 786436
  13.6 10.4 %copy-start.10 = (bf16[256,256]{1,0:T(8,128)(2,1)S(1)}, bf16[256,256]{1,0:T(8,128)(2,1)}, u32[]{:S(2)}) copy-start(bf16[256,256]{1,0:T(8,128)(2,1)} %constant.45.clone.wy_f) | copy-start | bytes 393220
  13.7 10.4 %copy-start.11 = (bf16[256,256]{1,0:T(8,128)(2,1)S(1)}, bf16[256,256]{1,0:T(8,128)(2,1)}, u32[]{:S(2)}) copy-start(bf16[256,256]{1,0:T(8,128)(2,1)} %constant.43.clone.wy_d) | copy-start | bytes 393220
  13.7 10.4 %copy-start.14 = (f32[48,128]{1,0:T(8,128)S(1)}, f32[48,128]{1,0:T(8,128)}, u32[]{:S(2)}) copy-start(f32[48,128]{1,0:T(8,128)} %constant.55.clone.fs_high) | copy-start | bytes 73732
  13.7 10.4 %copy-start.15 = (f32[48,128]{1,0:T(8,128)S(1)}, f32[48,128]{1,0:T(8,128)}, u32[]{:S(2)}) copy-start(f32[48,128]{1,0:T(8,128)} %constant.54.clone.fs_low) | copy-start | bytes 73732
  13.7 10.4 %copy-start.16 = (f32[4,8,128]{2,1,0:T(8,128)S(1)}, f32[4,8,128]{2,1,0:T(8,128)}, u32[]{:S(2)}) copy-start(f32[4,8,128]{2,1,0:T(8,128)} %constant.57.clone.fc_high) | copy-start | bytes 49156
  13.7 10.4 %copy-start.17 = (f32[4,8,128]{2,1,0:T(8,128)S(1)}, f32[4,8,128]{2,1,0:T(8,128)}, u32[]{:S(2)}) copy-start(f32[4,8,128]{2,1,0:T(8,128)} %constant.56.clone.fc_low) | copy-start | bytes 49156
  13.7 10.4 %copy-start.18 = (f32[24,128]{1,0:T(8,128)S(1)}, f32[24,128]{1,0:T(8,128)}, u32[]{:S(2)}) copy-start(f32[24,128]{1,0:T(8,128)} %constant.59.clone.ds_high) | copy-start | bytes 36868
  13.7 10.4 %copy-start.19 = (f32[24,128]{1,0:T(8,128)S(1)}, f32[24,128]{1,0:T(8,128)}, u32[]{:S(2)}) copy-start(f32[24,128]{1,0:T(8,128)} %constant.58.clone.ds_low) | copy-start | bytes 36868
  13.7 10.4 %copy-start.20 = (f32[8,128]{1,0:T(8,128)S(1)}, f32[8,128]{1,0:T(8,128)}, u32[]{:S(2)}) copy-start(f32[8,128]{1,0:T(8,128)} %constant.61.clone.dc_high) | copy-start | bytes 12292
  13.8 10.4 %copy-start.21 = (f32[8,128]{1,0:T(8,128)S(1)}, f32[8,128]{1,0:T(8,128)}, u32[]{:S(2)}) copy-start(f32[8,128]{1,0:T(8,128)} %constant.60.clone.dc_low) | copy-start | bytes 12292
  13.8 17.4 %collective-permute-start.3 = (f32[6,40,256]{2,1,0:T(8,128)S(1)}, f32[6,40,256]{2,1,0:T(8,128)S(1)}, u32[]{:S(2)}, u32[]{:S(2)}) collective-permute-start(f32[6,40,256]{2,1,0:T(8,128)S(1)} %get-tuple-element.18), channel_id=1, source_target_pairs={{0,15},{1,0},{2,1},{3,2},{4,3},{5,4},{6,5},{7,6},{8,7},{9,8},{10,9... | collective-permute-start | bytes 737288 | tf_op jit(solution)/shard_map/ppermute | solution.py:349
  21.9 9.2 %copy-start.2 = (bf16[128,512]{1,0:T(8,128)(2,1)S(1)}, bf16[128,512]{1,0:T(8,128)(2,1)}, u32[]{:S(2)}) copy-start(bf16[128,512]{1,0:T(8,128)(2,1)} %constant.53.clone.ux) | copy-start | bytes 393220
  22.0 9.2 %copy-start.5 = (bf16[48,256]{1,0:T(8,128)(2,1)S(1)}, bf16[48,256]{1,0:T(8,128)(2,1)}, u32[]{:S(2)}) copy-start(bf16[48,256]{1,0:T(8,128)(2,1)} %constant.62.clone.v) | copy-start | bytes 73732
  22.0 8.8 %collective-permute-start.5 = (f32[40,128]{1,0:T(8,128)S(1)}, f32[40,128]{1,0:T(8,128)S(1)}, u32[]{:S(2)}, u32[]{:S(2)}) collective-permute-start(f32[40,128]{1,0:T(8,128)S(1)} %corners.1), channel_id=1, source_target_pairs={{0,15},{1,0},{2,1},{3,2},{4,3},{5,4},{6,5},{7,6},{8,7},{9,8},{10,9... | collective-permute-start | bytes 61448 | tf_op jit(solution)/shard_map/ppermute | solution.py:349
  24.1 7.1 %collective-permute-start.4 = (f32[40,128]{1,0:T(8,128)S(1)}, f32[40,128]{1,0:T(8,128)S(1)}, u32[]{:S(2)}, u32[]{:S(2)}) collective-permute-start(f32[40,128]{1,0:T(8,128)S(1)} %corners.1), channel_id=1, source_target_pairs={{0,1},{1,2},{2,3},{3,4},{4,5},{5,6},{6,7},{7,8},{8,9},{9,10},{10,1... | collective-permute-start | bytes 61448 | tf_op jit(solution)/shard_map/ppermute | solution.py:349
  (6 other events, 6.2 us)

commit v2 on v1

v2 whole, which is shorter than its diff:
```python
import math

import jax
import jax.numpy as jnp
import ml_dtypes
import numpy as np
from jax import lax
from jax.experimental import pallas as pl
from jax.experimental.pallas import tpu as pltpu
from jax.sharding import PartitionSpec as P

F32 = jnp.float32
BF16 = jnp.bfloat16
deriv_offdiag = 1.0 / 3.0
coef_near = 14.0 / 9.0
coef_far = 1.0 / 9.0
filter_offdiag = 0.45
reach = 64
filter_rim = 48
deriv_rim = 24
group = 8


def filter_weights():
    return [
        (193.0 + 126.0 * filter_offdiag) / 256.0,
        (105.0 + 302.0 * filter_offdiag) / 256.0,
        15.0 * (2.0 * filter_offdiag - 1.0) / 64.0,
        45.0 * (1.0 - 2.0 * filter_offdiag) / 512.0,
        5.0 * (2.0 * filter_offdiag - 1.0) / 256.0,
        (1.0 - 2.0 * filter_offdiag) / 512.0,
    ]


class Line:
    def __init__(self, offdiag, taps, sign, width):
        gap = math.sqrt(1.0 - 4.0 * offdiag * offdiag)
        self.ratio = (gap - 1.0) / (2.0 * offdiag)
        self.gap = gap
        self.taps = taps
        self.sign = sign
        far = width + 4
        self.scale = self.tap(far) / self.ratio**far
        self.near = [0.0] + [
            self.tap(n) - self.scale * self.ratio**n if n <= width else 0.0 for n in range(1, 2 * far)
        ]

    def tap(self, n):
        return sum(w * self.ratio ** abs(n - o) / self.gap for o, w in self.taps)

    def block(self, cells):
        values = np.array([self.tap(n) for n in range(-cells + 1, cells)])
        ids = np.arange(cells)
        return values[ids[None, :] - ids[:, None] + cells - 1]

    def near_at(self, n):
        return self.near[n] if 0 < n < len(self.near) else 0.0

    def from_below(self, cells):
        table = np.zeros((cells, 5))
        for i in range(cells):
            table[i, 0] = self.sign * self.scale * self.ratio ** (i + 1)
            for k in range(4):
                table[i, 1 + k] = self.sign * self.near_at(i + 4 - k)
        return table

    def from_above(self, cells):
        table = np.zeros((cells, 5))
        for i in range(cells):
            table[i, 0] = self.scale * self.ratio ** (cells - i)
            for k in range(4):
                table[i, 1 + k] = self.near_at(cells + k - i)
        return table


def line_operators():
    weights = filter_weights()
    deriv_taps = [
        (-2, -coef_far / 4.0),
        (-1, -coef_near / 2.0),
        (1, coef_near / 2.0),
        (2, coef_far / 4.0),
    ]
    filter_taps = [(0, weights[0])]
    for order in range(1, 6):
        filter_taps.append((order, weights[order] / 2.0))
        filter_taps.append((-order, weights[order] / 2.0))
    return Line(deriv_offdiag, deriv_taps, -1.0, 1), Line(filter_offdiag, filter_taps, 1.0, 4)


def halves(table):
    hi = np.asarray(table, np.float32).astype(ml_dtypes.bfloat16)
    lo = (np.asarray(table, np.float64) - hi.astype(np.float64)).astype(ml_dtypes.bfloat16)
    return hi, lo


def split(values):
    hi = values.astype(BF16)
    return hi, (values - hi.astype(F32)).astype(BF16)


def dot(a, b, dims=((1,), (0,))):
    return lax.dot_general(a, b, (dims, ((), ())), preferred_element_type=F32)


def lanes(column):
    return np.repeat(np.asarray(column, np.float32)[:, None], 128, axis=1)


VMEM = pl.BlockSpec(memory_space=pltpu.VMEM)
ANY = pl.BlockSpec(memory_space=pl.ANY)


def call(name, kernel, outs, ins, flops, nbytes, in_specs=None, out_specs=None, scratch=(), limit=20, aliases=None):
    return pl.pallas_call(
        kernel,
        in_specs=in_specs or [VMEM] * len(ins),
        out_specs=out_specs or [VMEM] * len(outs),
        out_shape=[jax.ShapeDtypeStruct(shape, F32) for shape in outs],
        scratch_shapes=list(scratch),
        input_output_aliases=aliases or {},
        compiler_params=pltpu.CompilerParams(vmem_limit_bytes=limit << 20),
        cost_estimate=pl.CostEstimate(flops=flops, bytes_accessed=nbytes, transcendentals=0),
        name=name,
    )(*ins)


def powers_of(ratio, exponent, bits):
    out = jnp.where(exponent & 1 == 1, F32(ratio), F32(1.0))
    for b in range(1, bits):
        out = out * jnp.where((exponent >> b) & 1 == 1, F32(ratio ** (1 << b)), F32(1.0))
    return out


def y_functionals(cols):
    deriv, smooth = line_operators()
    shape = (8, cols)
    at = lax.broadcasted_iota(jnp.int32, shape, 1)
    row = lax.broadcasted_iota(jnp.int32, shape, 0)
    parts = []
    for place, first in ((at, at - (row - 1)), (cols - 1 - at, at - (cols - 5 + row))):
        cell = jnp.where((first == 0) & (row >= 1) & (row <= 4), F32(1.0), F32(0.0))
        cell = jnp.where(row == 0, powers_of(smooth.ratio, place, 7), cell)
        parts.append(jnp.where(row == 5, powers_of(deriv.ratio, place, 7), cell))
    hi, lo = split(jnp.concatenate(parts, axis=0))
    return jnp.concatenate(
        [jnp.concatenate([hi, hi], axis=1), jnp.concatenate([lo, jnp.zeros_like(lo)], axis=1)], axis=0
    )


def geometric(values, ratio, weights, tail):
    tiles = [values[8 * j : 8 * j + 8] for j in range(values.shape[0] // 8)]
    if not tail:
        tiles = tiles[::-1]
    total = tiles[0]
    for tile in tiles[1:]:
        total = total * F32(ratio**8) + tile
    return jnp.sum(total * weights, axis=0, keepdims=True)


def face_kernel(f_hbm, f, y_down, y_up, sems):
    planes, _, cols = f.shape
    steps = planes // group
    for i in range(steps):
        part = pl.ds(i * group, group)
        pltpu.make_async_copy(f_hbm.at[part], f.at[part], sems.at[i]).start()
    ty = y_functionals(cols)

    def step(i, carry):
        part = pl.ds(i * group, group)
        pltpu.make_async_copy(f_hbm.at[part], f.at[part], sems.at[i]).wait()
        for j in range(group):
            p = i * group + j
            row = pl.ds(p, 1)
            both = jnp.concatenate(split(f[p]), axis=-1)
            r = dot(ty, both, ((1,), (1,)))
            r = r[:16] + r[16:]
            for k in range(6):
                y_down[k, row, :] = r[k : k + 1]
                y_up[k, row, :] = r[8 + k : 9 + k]
        return carry

    lax.fori_loop(0, steps, step, 0)


def x_local_kernel(f, w, dx_out, fx, dx_low, dx_high, x_down, x_up, dx, sems):
    planes, n, cols = f.shape
    pairs = group // 2
    deriv, smooth = line_operators()
    at = lax.broadcasted_iota(jnp.int32, (8, cols), 0)
    f_head, f_tail = powers_of(smooth.ratio, at, 3), powers_of(smooth.ratio, 7 - at, 3)
    d_head, d_tail = powers_of(deriv.ratio, at, 3), powers_of(deriv.ratio, 7 - at, 3)
    inner = pl.ds(deriv_rim, n - 2 * deriv_rim)

    def written(i):
        part = pl.ds(i * group, group)
        return pltpu.make_async_copy(dx.at[part, inner], dx_out.at[part, inner], sems.at[i])

    def step(i, carry):
        for j in range(pairs):
            p = i * group + 2 * j
            hi, lo = split(jnp.concatenate([f[p], f[p + 1]], axis=-1))
            r = dot(w[:, :n], hi) + dot(w[:, n:], hi) + dot(w[:, :n], lo)
            for half in range(2):
                q = p + half
                at = slice(128 * half, 128 * half + 128)
                dx[q] = r[:n, at]
                dx_low[q] = r[:deriv_rim, at]
                dx_high[q] = r[n - deriv_rim : n, at]
                fx[q] = r[n:, at]
                row = pl.ds(q, 1)
                x_down[0, row, :] = geometric(f[q, :reach, :], smooth.ratio, f_head, False)
                x_up[0, row, :] = geometric(f[q, n - reach :, :], smooth.ratio, f_tail, True)
                x_down[5, row, :] = geometric(f[q, : reach // 2, :], deriv.ratio, d_head, False)
                x_up[5, row, :] = geometric(f[q, n - reach // 2 :, :], deriv.ratio, d_tail, True)
                for k in range(4):
                    x_down[1 + k, row, :] = f[q, k : k + 1, :]
                    x_up[1 + k, row, :] = f[q, n - 4 + k : n - 3 + k, :]
        written(i).start()
        return carry

    lax.fori_loop(0, planes // group, step, 0)
    for i in range(planes // group):
        written(i).wait()


def dot3(rows, hi, lo):
    a, b = split(rows)
    return dot(a, hi) + dot(a, lo) + dot(b, hi)


def x_face_kernel(x_down, x_up, lower, upper, by, tx, vy, down, up):
    planes = lower.shape[1]
    n = by.shape[1] // 2
    rows = jnp.concatenate([x_down[k] for k in range(5)] + [x_up[k] for k in range(5)], axis=0)
    own = dot3(rows, by[:, :n], by[:, n:])
    rows = jnp.concatenate([lower[g] for g in range(5)] + [upper[g] for g in range(5)], axis=0)
    r = dot3(rows, tx[:, :128], tx[:, 128:])
    z = r[:planes]
    for g in range(1, 10):
        z = z + pltpu.roll(r[g * planes : (g + 1) * planes], 10 * g, 1)
    rows = jnp.concatenate([z] + [pltpu.roll(z, 128 - k, 1) for k in range(1, 10)], axis=0)
    own = own + dot3(rows, vy[:, :n], vy[:, n:])
    for k in range(5):
        down[k] = own[k * planes : (k + 1) * planes]
        up[k] = own[(5 + k) * planes : (6 + k) * planes]
    down[5] = x_down[5]
    up[5] = x_up[5]
    down[6] = x_down[1]
    up[6] = x_up[4]


def y_kernel(f, fx, lower, upper, ax, v, wy_d, wy_f, dy_out, sm_out, sm_low, sm_high, halo, dy, sm, sems):
    planes, n, _ = f.shape
    rows = jnp.concatenate([lower[k] for k in range(5)] + [upper[k] for k in range(5)], axis=0)
    filtered = dot3(rows, ax[:, :n], ax[:, n:])
    zero = jnp.zeros((planes, n), F32)
    table = [filtered[k * planes : (k + 1) * planes] for k in range(5)] + [lower[5], lower[4], zero]
    table += [filtered[(5 + k) * planes : (6 + k) * planes] for k in range(5)] + [upper[5], upper[1], zero]
    for k in range(16):
        for c in range(0, n, 128):
            halo[c // 128, pl.ds(k, planes, stride=16), :] = table[k][:, c : c + 128]
    inner = pl.ds(filter_rim, n - 2 * filter_rim)

    def written(i):
        part = pl.ds(i * group, group)
        return (
            pltpu.make_async_copy(dy.at[part], dy_out.at[part], sems.at[0, i]),
            pltpu.make_async_copy(sm.at[part, inner], sm_out.at[part, inner], sems.at[1, i]),
        )

    def step(i, carry):
        for j in range(group):
            p = i * group + j
            at = pl.ds(pl.multiple_of(p * 16, 16), 16)
            hi, lo = split(jnp.concatenate([halo[c, at, :] for c in range(n // 128)], axis=-1))
            r = dot(jnp.concatenate([hi, lo, hi], axis=0), v[...], ((0,), (0,)))
            d = dot(jnp.concatenate(split(f[p]), axis=-1), wy_d[...])
            dy[p] = d[:, :128] + d[:, 128:] + r[:, :128]
            s = dot(jnp.concatenate(split(fx[p]), axis=-1), wy_f[...])
            s = s[:, :128] + s[:, 128:] + r[:, 128:]
            sm[p] = s
            sm_low[p] = s[:filter_rim]
            sm_high[p] = s[n - filter_rim :]
        for copy in written(i):
            copy.start()
        return carry

    lax.fori_loop(0, planes // group, step, 0)
    for i in range(planes // group):
        for copy in written(i):
            copy.wait()


def rim_kernel(
    dx_low, dx_high, sm_low, sm_high, lower, upper, ds_low, ds_high, dc_low, dc_high, fs_low, fs_high, fc_low, fc_high,
    dx_in, sm_in, dx_out, sm_out, dl, dh, sl, sh, sems,
):
    planes = dx_low.shape[0]
    n = dx_out.shape[1]

    def written(i):
        part = pl.ds(i * group, group)
        return (
            pltpu.make_async_copy(dl.at[part], dx_out.at[part, pl.ds(0, deriv_rim)], sems.at[0, i]),
            pltpu.make_async_copy(dh.at[part], dx_out.at[part, pl.ds(n - deriv_rim, deriv_rim)], sems.at[1, i]),
            pltpu.make_async_copy(sl.at[part], sm_out.at[part, pl.ds(0, filter_rim)], sems.at[2, i]),
            pltpu.make_async_copy(sh.at[part], sm_out.at[part, pl.ds(n - filter_rim, filter_rim)], sems.at[3, i]),
        )

    def step(i, carry):
        for j in range(group):
            p = i * group + j
            row = pl.ds(p, 1)
            low = dx_low[p] + ds_low[...] * lower[5, row, :]
            high = dx_high[p] + ds_high[...] * upper[5, row, :]
            dl[p] = jnp.concatenate([low[:8] + dc_low[...] * lower[6, row, :], low[8:]], axis=0)
            dh[p] = jnp.concatenate([high[:-8], high[-8:] + dc_high[...] * upper[6, row, :]], axis=0)
            low = sm_low[p] + fs_low[...] * lower[0, row, :]
            high = sm_high[p] + fs_high[...] * upper[0, row, :]
            near_low, near_high = low[:8], high[-8:]
            for k in range(4):
                near_low = near_low + fc_low[k] * lower[1 + k, row, :]
                near_high = near_high + fc_high[k] * upper[1 + k, row, :]
            sl[p] = jnp.concatenate([near_low, low[8:]], axis=0)
            sh[p] = jnp.concatenate([high[:-8], near_high], axis=0)
        for copy in written(i):
            copy.start()
        return carry

    lax.fori_loop(0, planes // group, step, 0)
    for i in range(planes // group):
        for copy in written(i):
            copy.wait()


def tables(rows, cols):
    deriv, smooth = line_operators()
    t = {}
    for name, line in (("d", deriv), ("f", smooth)):
        hi, lo = halves(line.block(rows))
        t["wx_" + name] = np.concatenate([hi, lo], axis=1)
        hi, lo = halves(line.block(cols).T)
        t["wy_" + name] = np.block([[hi, lo], [hi, np.zeros_like(lo)]])
    hi, lo = halves(smooth.block(rows).T)
    t["ax"] = np.concatenate([hi, lo], axis=1)
    t["wx"] = np.concatenate([t.pop("wx_d"), t.pop("wx_f")], axis=0)
    powers = lambda line, count: line.ratio ** np.arange(count)
    hi, lo = halves(smooth.block(cols).T)
    t["by"] = np.concatenate([hi, lo], axis=1)
    tx = np.zeros((rows, 128))
    tx[:, 0] = powers(smooth, rows)
    tx[:, 5] = tx[::-1, 0]
    for k in range(4):
        tx[k, 1 + k] = 1.0
        tx[rows - 4 + k, 6 + k] = 1.0
    hi, lo = halves(tx)
    t["tx"] = np.concatenate([hi, lo], axis=1)
    low, high = smooth.from_below(cols), smooth.from_above(cols)
    vy = np.zeros((128, cols))
    for g in range(5):
        vy[10 * g] = low[:, g]
        vy[10 * (5 + g)] = high[:, g]
    hi, lo = halves(vy)
    t["vy"] = np.concatenate([hi, lo], axis=1)
    low, high = smooth.from_below(rows), smooth.from_above(rows)
    t["fs_low"], t["fs_high"] = lanes(low[:filter_rim, 0]), lanes(high[-filter_rim:, 0])
    t["fc_low"] = np.stack([lanes(low[:8, 1 + k]) for k in range(4)])
    t["fc_high"] = np.stack([lanes(high[-8:, 1 + k]) for k in range(4)])
    low, high = deriv.from_below(rows), deriv.from_above(rows)
    t["ds_low"], t["ds_high"] = lanes(low[:deriv_rim, 0]), lanes(high[-deriv_rim:, 0])
    t["dc_low"], t["dc_high"] = lanes(low[:8, 4]), lanes(high[-8:, 1])
    v = np.zeros((16, 2 * cols))
    low, high = smooth.from_below(cols), smooth.from_above(cols)
    v[0:5, cols:], v[8:13, cols:] = low.T, high.T
    low, high = deriv.from_below(cols), deriv.from_above(cols)
    v[5, :cols], v[6, :cols] = low[:, 0], low[:, 4]
    v[13, :cols], v[14, :cols] = high[:, 0], high[:, 1]
    hi, lo = halves(v)
    t["v"] = np.concatenate([hi, hi, lo], axis=0)
    return {key: jnp.asarray(value) for key, value in t.items()}


def shifted(values, axis, by):
    count = lax.axis_size(axis)
    return lax.ppermute(values, axis, [(i, (i + by) % count) for i in range(count)])


def on_device(fields):
    shape = fields.shape
    rows, cols = shape[2:]
    planes = shape[0] * shape[1]
    block = (planes, rows, cols)
    t = tables(rows, cols)
    steps = planes // group
    x_face, y_face = (6, planes, cols), (6, planes, rows)
    dx_rim, sm_rim = (planes, deriv_rim, cols), (planes, filter_rim, cols)
    f, y_down, y_up = call(
        "faces", face_kernel, [block, y_face, y_face],
        [pltpu.with_memory_space_constraint(fields.reshape(block), pltpu.HBM)], 10**9, 10**7,
        in_specs=[ANY], scratch=[pltpu.SemaphoreType.DMA((steps,))],
    )
    y_lower = shifted(y_up, "gy", 1)
    y_upper = shifted(y_down, "gy", -1)
    dx, fx, dx_low, dx_high, x_down, x_up = call(
        "x_local", x_local_kernel, [block, block, dx_rim, dx_rim, x_face, x_face], [f, t["wx"]], 4 * 10**9, 10**7,
        out_specs=[ANY] + [VMEM] * 5,
        scratch=[pltpu.VMEM(block, F32), pltpu.SemaphoreType.DMA((steps,))],
    )
    face = (7, planes, cols)
    x_down, x_up = call(
        "x_faces", x_face_kernel, [face, face],
        [x_down, x_up, y_lower, y_upper, t["by"], t["tx"], t["vy"]], 10**8, 10**6,
    )
    x_lower = shifted(x_up, "gx", 1)
    x_upper = shifted(x_down, "gx", -1)
    dy, sm, sm_low, sm_high = call(
        "y_all", y_kernel, [block, block, sm_rim, sm_rim],
        [f, fx, y_lower, y_upper] + [t[k] for k in ("ax", "v", "wy_d", "wy_f")], 6 * 10**9, 2 * 10**7,
        out_specs=[ANY, ANY, VMEM, VMEM],
        scratch=[
            pltpu.VMEM((rows // 128, planes * 16, 128), F32),
            pltpu.VMEM(block, F32),
            pltpu.VMEM(block, F32),
            pltpu.SemaphoreType.DMA((2, steps)),
        ],
        limit=24,
    )
    rims = ("ds_low", "ds_high", "dc_low", "dc_high", "fs_low", "fs_high", "fc_low", "fc_high")
    ins = [dx_low, dx_high, sm_low, sm_high, x_lower, x_upper] + [t[k] for k in rims]
    dx, sm = call(
        "rims", rim_kernel, [block, block], ins + [dx, sm], 10**8, 4 * 10**6,
        in_specs=[VMEM] * len(ins) + [ANY, ANY],
        out_specs=[ANY, ANY],
        scratch=[pltpu.VMEM(shape, F32) for shape in (dx_rim, dx_rim, sm_rim, sm_rim)]
        + [pltpu.SemaphoreType.DMA((4, steps))],
        aliases={len(ins): 0, len(ins) + 1: 1},
    )
    return tuple(out.reshape(shape) for out in (dx, dy, sm))


def solution(mesh):
    placed = P(None, None, "gx", "gy")
    return jax.shard_map(
        on_device, mesh=mesh, in_specs=(placed,), out_specs=(placed, placed, placed), check_vma=False
    )
```

time: 36.8 us -> 30.2 us (0.82)
  local copies, waits for them, and re-layouts: 6.25 us -> 0.1 us
  Pallas kernels: 17.4 us -> 19.6 us
  starting transfers between devices: 11.5 us -> 9.43 us
    unnamed x48 -> x32, local copies, waits for them, and re-layouts: 6.25 us -> 0.1 us
    pallas_call x5, Pallas kernels: 17.4 us -> 19.6 us  [call(): pl.pallas_call(kernel, in_specs=in_specs or [VMEM] * len(ins), out_specs=...]
    ppermute x6 -> x4, starting transfers between devices: 11.5 us -> 9.43 us  [shifted(): lax.ppermute(values, axis, [(i, (i + by) % count) for i in range(count)])]
  transfers between devices with their start and end apart: 6 -> 4, of which waited for: 1 -> 0; matrix products, arithmetic and copies ran while one was open for 0% -> 0% of each run, Pallas kernels for 27% -> 44%
where the time goes in v2:
time: 30.2 us; the launch traced here: 30.1 us
  Pallas kernels  19.6 us (65%)
  starting transfers between devices  9.43 us (31%)
  between operations  0.9 us (3%)
    pallas_call x5, Pallas kernels, call(): pl.pallas_call(kernel, in_specs=in_specs or [VMEM] * len(ins), out_specs=...  19.6 us
    ppermute x4, starting transfers between devices, shifted(): lax.ppermute(values, axis, [(i, (i + by) % count) for i in range(count)])  9.43 us
  transfers between devices with their start and end apart: 4, of which 0 were waited for; matrix products, arithmetic and copies ran while one was open for 0% of the time, Pallas kernels for 44%

profile of v2, /device:TPU:0, one launch (start us, length us, event | category | flops | bytes accessed | tf_op | source)
XLA Modules:
  0.0 30.1 jit_solution(3443591812401149652)
XLA Ops:
  0.6 0.0 copy-start.11
  0.6 3.5 %faces.1 = (f32[40,256,128]{2,1,0:T(8,128)S(1)}, f32[6,40,256]{2,1,0:T(8,128)S(1)}, f32[6,40,256]{2,1,0:T(8,128)S(1)}) custom-call(f32[40,256,128]{2,1,0:T(8,128)} %bitcast.4), custom_call_target="tpu_custom_call" | custom-call | flops 1000000000 | bytes 10000000 | tf_op jit(solution)/shard_map/faces/pallas_call | solution.py:115
  4.1 1.6 %collective-permute-start = (f32[6,40,256]{2,1,0:T(8,128)S(1)}, f32[6,40,256]{2,1,0:T(8,128)S(1)}, u32[]{:S(2)}, u32[]{:S(2)}) collective-permute-start(f32[6,40,256]{2,1,0:T(8,128)S(1)} %get-tuple-element.24), channel_id=1, source_target_pairs={{0,1},{1,2},{2,3},{3,4},{4,5},{5,6},{6,7},{7,8},{8,9},{9,10},{10,1... | collective-permute-start | bytes 737288 | tf_op jit(solution)/shard_map/ppermute | solution.py:386
  5.8 4.8 %collective-permute-start.1 = (f32[6,40,256]{2,1,0:T(8,128)S(1)}, f32[6,40,256]{2,1,0:T(8,128)S(1)}, u32[]{:S(2)}, u32[]{:S(2)}) collective-permute-start(f32[6,40,256]{2,1,0:T(8,128)S(1)} %get-tuple-element.25), channel_id=1, source_target_pairs={{0,15},{1,0},{2,1},{3,2},{4,3},{5,4},{6,5},{7,6},{8,7},{9,8},{10,9... | collective-permute-start | bytes 737288 | tf_op jit(solution)/shard_map/ppermute | solution.py:386
  10.6 0.0 copy-start.12
  10.6 0.0 copy-start.13
  10.6 0.0 copy-start.14
  10.7 0.0 copy-start.15
  10.7 6.2 %x_local.1 = (f32[40,256,128]{2,1,0:T(8,128)}, f32[40,256,128]{2,1,0:T(8,128)S(1)}, f32[40,24,128]{2,1,0:T(8,128)S(1)}, f32[40,24,128]{2,1,0:T(8,128)S(1)}, f32[...) custom-call(f32[40,256,128]{2,1,0:T(8,128)S(1)} %get-tuple-element.20.f, bf16[512,512]{1,0:T(8,128)(2,1)S(1)} %copy-done.11), custom_call_target="tpu_custom_call" | custom-call | flops 4000000000 | bytes 10000000 | tf_op jit(solution)/shard_map/x_local/pallas_call | solution.py:115
  16.9 0.0 collective-permute-done.lower
  16.9 1.2 %x_faces.1 = (f32[7,40,128]{2,1,0:T(8,128)S(1)}, f32[7,40,128]{2,1,0:T(8,128)S(1)}) custom-call(f32[6,40,128]{2,1,0:T(8,128)S(1)} %get-tuple-element.28.x_down, f32[6,40,128]{2,1,0:T(8,128)S(1)} %get-tuple-element.29.x_up, f32[6,40,256]{2,1,0:T(8,128)S(1)} %collective-permute-done.lower, f32[6,40,256]{2,1,0:T(8,128)S(1)} %collective-permute-done.1.upper, ...), custom_call_target="tpu_custom_call" | custom-call | flops 100000000 | bytes 1000000 | tf_op jit(solution)/shard_map/x_faces/pallas_call | solution.py:115
  18.1 0.0 collective-permute-start.2
  18.1 2.9 %collective-permute-start.3 = (f32[7,40,128]{2,1,0:T(8,128)S(1)}, f32[7,40,128]{2,1,0:T(8,128)S(1)}, u32[]{:S(2)}, u32[]{:S(2)}) collective-permute-start(f32[7,40,128]{2,1,0:T(8,128)S(1)} %get-tuple-element.31), channel_id=1, source_target_pairs={{0,112},{16,0},{32,16},{48,32},{64,48},{80,64},{96,80},{112,96},{1... | collective-permute-start | bytes 430088 | tf_op jit(solution)/shard_map/ppermute | solution.py:386
  21.1 0.0 copy-start.3
  21.1 0.0 copy-start.4
  21.1 0.0 copy-start.5
  21.1 0.0 copy-start.6
  21.1 0.0 copy-start.7
  21.1 0.0 copy-start.8
  21.2 0.0 copy-start.9
  21.2 0.0 copy-start.10
  21.2 7.0 %y_all.1 = (f32[40,256,128]{2,1,0:T(8,128)}, f32[40,256,128]{2,1,0:T(8,128)}, f32[40,48,128]{2,1,0:T(8,128)S(1)}, f32[40,48,128]{2,1,0:T(8,128)S(1)}) custom-call(f32[40,256,128]{2,1,0:T(8,128)S(1)} %get-tuple-element.20.f, f32[40,256,128]{2,1,0:T(8,128)S(1)} %get-tuple-element.23.fx, f32[6,40,256]{2,1,0:T(8,128)S(1)} %collective-permute-done.lower, ...), custom_call_target="tpu_custom_call" | custom-call | flops 6000000000 | bytes 20000000 | tf_op jit(solution)/shard_map/y_all/pallas_call | solution.py:115
  28.2 0.0 collective-permute-done.3.upper
  28.3 1.8 %rims.1 = (f32[40,256,128]{2,1,0:T(8,128)}, f32[40,256,128]{2,1,0:T(8,128)}) custom-call(f32[40,24,128]{2,1,0:T(8,128)S(1)} %get-tuple-element.21.dx_low, f32[40,24,128]{2,1,0:T(8,128)S(1)} %get-tuple-element.22.dx_high, f32[40,48,128]{2,1,0:T(8,128)S(1)} %get-tuple-element.26.sm_low, ...), custom_call_target="tpu_custom_call", output_to_operand_aliasing={{0}: (14, {}), {1}: (15, {})} | custom-call | flops 100000000 | bytes 4000000 | tf_op jit(solution)/shard_map/rims/pallas_call | solution.py:115
  (21 shorter events, 0.0 us)
Async XLA Ops:
  0.6 10.0 %copy-start.11 = (bf16[512,512]{1,0:T(8,128)(2,1)S(1)}, bf16[512,512]{1,0:T(8,128)(2,1)}, u32[]{:S(2)}) copy-start(bf16[512,512]{1,0:T(8,128)(2,1)} %constant.35.clone.w) | copy-start | bytes 1572868
  4.1 12.7 %collective-permute-start = (f32[6,40,256]{2,1,0:T(8,128)S(1)}, f32[6,40,256]{2,1,0:T(8,128)S(1)}, u32[]{:S(2)}, u32[]{:S(2)}) collective-permute-start(f32[6,40,256]{2,1,0:T(8,128)S(1)} %get-tuple-element.24), channel_id=1, source_target_pairs={{0,1},{1,2},{2,3},{3,4},{4,5},{5,6},{6,7},{7,8},{8,9},{9,10},{10,1... | collective-permute-start | bytes 737288 | tf_op jit(solution)/shard_map/ppermute | solution.py:386
  5.8 11.1 %collective-permute-start.1 = (f32[6,40,256]{2,1,0:T(8,128)S(1)}, f32[6,40,256]{2,1,0:T(8,128)S(1)}, u32[]{:S(2)}, u32[]{:S(2)}) collective-permute-start(f32[6,40,256]{2,1,0:T(8,128)S(1)} %get-tuple-element.25), channel_id=1, source_target_pairs={{0,15},{1,0},{2,1},{3,2},{4,3},{5,4},{6,5},{7,6},{8,7},{9,8},{10,9... | collective-permute-start | bytes 737288 | tf_op jit(solution)/shard_map/ppermute | solution.py:386
  10.6 6.3 %copy-start = (bf16[256,256]{1,0:T(8,128)(2,1)S(1)}, bf16[256,256]{1,0:T(8,128)(2,1)}, u32[]{:S(2)}) copy-start(bf16[256,256]{1,0:T(8,128)(2,1)} %constant.37.clone.tx) | copy-start | bytes 393220
  10.6 6.3 %copy-start.1 = (bf16[128,256]{1,0:T(8,128)(2,1)S(1)}, bf16[128,256]{1,0:T(8,128)(2,1)}, u32[]{:S(2)}) copy-start(bf16[128,256]{1,0:T(8,128)(2,1)} %constant.36.clone.by) | copy-start | bytes 196612
  10.6 6.3 %copy-start.2 = (bf16[128,256]{1,0:T(8,128)(2,1)S(1)}, bf16[128,256]{1,0:T(8,128)(2,1)}, u32[]{:S(2)}) copy-start(bf16[128,256]{1,0:T(8,128)(2,1)} %constant.38.clone.vy) | copy-start | bytes 196612
  10.6 10.5 %copy-start.12 = (bf16[256,512]{1,0:T(8,128)(2,1)S(1)}, bf16[256,512]{1,0:T(8,128)(2,1)}, u32[]{:S(2)}) copy-start(bf16[256,512]{1,0:T(8,128)(2,1)} %constant.34.clone.ax) | copy-start | bytes 786436
  10.6 10.5 %copy-start.13 = (bf16[256,256]{1,0:T(8,128)(2,1)S(1)}, bf16[256,256]{1,0:T(8,128)(2,1)}, u32[]{:S(2)}) copy-start(bf16[256,256]{1,0:T(8,128)(2,1)} %constant.32.clone.wy_d) | copy-start | bytes 393220
  10.6 10.4 %copy-start.14 = (bf16[256,256]{1,0:T(8,128)(2,1)S(1)}, bf16[256,256]{1,0:T(8,128)(2,1)}, u32[]{:S(2)}) copy-start(bf16[256,256]{1,0:T(8,128)(2,1)} %constant.33.clone.wy_f) | copy-start | bytes 393220
  10.7 10.4 %copy-start.15 = (bf16[48,256]{1,0:T(8,128)(2,1)S(1)}, bf16[48,256]{1,0:T(8,128)(2,1)}, u32[]{:S(2)}) copy-start(bf16[48,256]{1,0:T(8,128)(2,1)} %constant.47.clone.v) | copy-start | bytes 73732
  18.1 10.1 %collective-permute-start.2 = (f32[7,40,128]{2,1,0:T(8,128)S(1)}, f32[7,40,128]{2,1,0:T(8,128)S(1)}, u32[]{:S(2)}, u32[]{:S(2)}) collective-permute-start(f32[7,40,128]{2,1,0:T(8,128)S(1)} %get-tuple-element.30), channel_id=1, source_target_pairs={{0,16},{16,32},{32,48},{48,64},{64,80},{80,96},{96,112},{112,0},{1... | collective-permute-start | bytes 430088 | tf_op jit(solution)/shard_map/ppermute | solution.py:386
  18.1 10.1 %collective-permute-start.3 = (f32[7,40,128]{2,1,0:T(8,128)S(1)}, f32[7,40,128]{2,1,0:T(8,128)S(1)}, u32[]{:S(2)}, u32[]{:S(2)}) collective-permute-start(f32[7,40,128]{2,1,0:T(8,128)S(1)} %get-tuple-element.31), channel_id=1, source_target_pairs={{0,112},{16,0},{32,16},{48,32},{64,48},{80,64},{96,80},{112,96},{1... | collective-permute-start | bytes 430088 | tf_op jit(solution)/shard_map/ppermute | solution.py:386
  21.1 7.1 %copy-start.3 = (f32[48,128]{1,0:T(8,128)S(1)}, f32[48,128]{1,0:T(8,128)}, u32[]{:S(2)}) copy-start(f32[48,128]{1,0:T(8,128)} %constant.39.clone.fs_low) | copy-start | bytes 73732
  21.1 7.1 %copy-start.4 = (f32[48,128]{1,0:T(8,128)S(1)}, f32[48,128]{1,0:T(8,128)}, u32[]{:S(2)}) copy-start(f32[48,128]{1,0:T(8,128)} %constant.40.clone.fs_high) | copy-start | bytes 73732
  21.1 7.1 %copy-start.5 = (f32[4,8,128]{2,1,0:T(8,128)S(1)}, f32[4,8,128]{2,1,0:T(8,128)}, u32[]{:S(2)}) copy-start(f32[4,8,128]{2,1,0:T(8,128)} %constant.41.clone.fc_low) | copy-start | bytes 49156
  21.1 7.1 %copy-start.6 = (f32[4,8,128]{2,1,0:T(8,128)S(1)}, f32[4,8,128]{2,1,0:T(8,128)}, u32[]{:S(2)}) copy-start(f32[4,8,128]{2,1,0:T(8,128)} %constant.42.clone.fc_high) | copy-start | bytes 49156
  21.1 7.1 %copy-start.7 = (f32[24,128]{1,0:T(8,128)S(1)}, f32[24,128]{1,0:T(8,128)}, u32[]{:S(2)}) copy-start(f32[24,128]{1,0:T(8,128)} %constant.43.clone.ds_low) | copy-start | bytes 36868
  21.1 7.1 %copy-start.8 = (f32[24,128]{1,0:T(8,128)S(1)}, f32[24,128]{1,0:T(8,128)}, u32[]{:S(2)}) copy-start(f32[24,128]{1,0:T(8,128)} %constant.44.clone.ds_high) | copy-start | bytes 36868
  21.2 7.1 %copy-start.9 = (f32[8,128]{1,0:T(8,128)S(1)}, f32[8,128]{1,0:T(8,128)}, u32[]{:S(2)}) copy-start(f32[8,128]{1,0:T(8,128)} %constant.45.clone.dc_low) | copy-start | bytes 12292
  21.2 7.1 %copy-start.10 = (f32[8,128]{1,0:T(8,128)S(1)}, f32[8,128]{1,0:T(8,128)}, u32[]{:S(2)}) copy-start(f32[8,128]{1,0:T(8,128)} %constant.46.clone.dc_high) | copy-start | bytes 12292

commit v3 on v2

v3 whole, which is shorter than its diff:
```python
import math

import jax
import jax.numpy as jnp
import ml_dtypes
import numpy as np
from jax import lax
from jax.experimental import pallas as pl
from jax.experimental.pallas import tpu as pltpu
from jax.sharding import PartitionSpec as P

F32 = jnp.float32
BF16 = jnp.bfloat16
deriv_offdiag = 1.0 / 3.0
coef_near = 14.0 / 9.0
coef_far = 1.0 / 9.0
filter_offdiag = 0.45
reach = 64
filter_rim = 40
deriv_rim = 24
group = 8
pieces = ((0, 8), (8, 8), (16, 8), (24, 8), (32, 8))
span = 40
chunk = 4


def filter_weights():
    return [
        (193.0 + 126.0 * filter_offdiag) / 256.0,
        (105.0 + 302.0 * filter_offdiag) / 256.0,
        15.0 * (2.0 * filter_offdiag - 1.0) / 64.0,
        45.0 * (1.0 - 2.0 * filter_offdiag) / 512.0,
        5.0 * (2.0 * filter_offdiag - 1.0) / 256.0,
        (1.0 - 2.0 * filter_offdiag) / 512.0,
    ]


class Line:
    def __init__(self, offdiag, taps, sign, width):
        gap = math.sqrt(1.0 - 4.0 * offdiag * offdiag)
        self.ratio = (gap - 1.0) / (2.0 * offdiag)
        self.gap = gap
        self.taps = taps
        self.sign = sign
        far = width + 4
        self.scale = self.tap(far) / self.ratio**far
        self.near = [0.0] + [
            self.tap(n) - self.scale * self.ratio**n if n <= width else 0.0 for n in range(1, 2 * far)
        ]

    def tap(self, n):
        return sum(w * self.ratio ** abs(n - o) / self.gap for o, w in self.taps)

    def block(self, cells):
        values = np.array([self.tap(n) for n in range(-cells + 1, cells)])
        ids = np.arange(cells)
        return values[ids[None, :] - ids[:, None] + cells - 1]

    def near_at(self, n):
        return self.near[n] if 0 < n < len(self.near) else 0.0

    def from_below(self, cells):
        table = np.zeros((cells, 5))
        for i in range(cells):
            table[i, 0] = self.sign * self.scale * self.ratio ** (i + 1)
            for k in range(4):
                table[i, 1 + k] = self.sign * self.near_at(i + 4 - k)
        return table

    def from_above(self, cells):
        table = np.zeros((cells, 5))
        for i in range(cells):
            table[i, 0] = self.scale * self.ratio ** (cells - i)
            for k in range(4):
                table[i, 1 + k] = self.near_at(cells + k - i)
        return table


def line_operators():
    weights = filter_weights()
    deriv_taps = [
        (-2, -coef_far / 4.0),
        (-1, -coef_near / 2.0),
        (1, coef_near / 2.0),
        (2, coef_far / 4.0),
    ]
    filter_taps = [(0, weights[0])]
    for order in range(1, 6):
        filter_taps.append((order, weights[order] / 2.0))
        filter_taps.append((-order, weights[order] / 2.0))
    return Line(deriv_offdiag, deriv_taps, -1.0, 1), Line(filter_offdiag, filter_taps, 1.0, 4)


def halves(table):
    hi = np.asarray(table, np.float32).astype(ml_dtypes.bfloat16)
    lo = (np.asarray(table, np.float64) - hi.astype(np.float64)).astype(ml_dtypes.bfloat16)
    return hi, lo


def split(values):
    hi = values.astype(BF16)
    return hi, (values - hi.astype(F32)).astype(BF16)


def dot(a, b, dims=((1,), (0,))):
    return lax.dot_general(a, b, (dims, ((), ())), preferred_element_type=F32)


def lanes(column):
    return np.repeat(np.asarray(column, np.float32)[:, None], 128, axis=1)


VMEM = pl.BlockSpec(memory_space=pltpu.VMEM)
ANY = pl.BlockSpec(memory_space=pl.ANY)


def call(name, kernel, outs, ins, flops, nbytes, in_specs=None, out_specs=None, scratch=(), limit=20, aliases=None):
    return pl.pallas_call(
        kernel,
        in_specs=in_specs or [VMEM] * len(ins),
        out_specs=out_specs or [VMEM] * len(outs),
        out_shape=[jax.ShapeDtypeStruct(shape, F32) for shape in outs],
        scratch_shapes=list(scratch),
        input_output_aliases=aliases or {},
        compiler_params=pltpu.CompilerParams(vmem_limit_bytes=limit << 20),
        cost_estimate=pl.CostEstimate(flops=flops, bytes_accessed=nbytes, transcendentals=0),
        name=name,
    )(*ins)


def powers_of(ratio, exponent, bits):
    out = jnp.where(exponent & 1 == 1, F32(ratio), F32(1.0))
    for b in range(1, bits):
        out = out * jnp.where((exponent >> b) & 1 == 1, F32(ratio ** (1 << b)), F32(1.0))
    return out


def y_functionals(cols):
    deriv, smooth = line_operators()
    shape = (8, cols)
    at = lax.broadcasted_iota(jnp.int32, shape, 1)
    row = lax.broadcasted_iota(jnp.int32, shape, 0)
    parts = []
    for place, first in ((at, at - (row - 1)), (cols - 1 - at, at - (cols - 5 + row))):
        cell = jnp.where((first == 0) & (row >= 1) & (row <= 4), F32(1.0), F32(0.0))
        cell = jnp.where(row == 0, powers_of(smooth.ratio, place, 7), cell)
        parts.append(jnp.where(row == 5, powers_of(deriv.ratio, place, 7), cell))
    hi, lo = split(jnp.concatenate(parts, axis=0))
    return jnp.concatenate(
        [jnp.concatenate([hi, hi], axis=1), jnp.concatenate([lo, jnp.zeros_like(lo)], axis=1)], axis=0
    )


def geometric(values, ratio, weights, tail):
    tiles = [values[8 * j : 8 * j + 8] for j in range(values.shape[0] // 8)]
    if not tail:
        tiles = tiles[::-1]
    total = tiles[0]
    for tile in tiles[1:]:
        total = total * F32(ratio**8) + tile
    return jnp.sum(total * weights, axis=0, keepdims=True)


def face_kernel(f_hbm, f, y_down, y_up, sems):
    cols = f.shape[2]
    reads = []
    for i, (first, planes) in enumerate(pieces):
        part = pl.ds(first, planes)
        reads.append(pltpu.make_async_copy(f_hbm.at[part], f.at[part], sems.at[i]))
        reads[-1].start()
    ty = y_functionals(cols)
    for read, (first, planes) in zip(reads, pieces):
        read.wait()
        for p in range(first, first + planes):
            both = jnp.concatenate(split(f[p]), axis=-1)
            r = dot(ty, both, ((1,), (1,)))
            r = r[:16] + r[16:]
            for k in range(6):
                y_down[k, p : p + 1, :] = r[k : k + 1]
                y_up[k, p : p + 1, :] = r[8 + k : 9 + k]


def windows(cells, margin):
    pieces, first = [], 0
    while first < cells:
        start = min(max(0, (first - margin) // 16 * 16), cells - 128)
        end = cells if start == cells - 128 else (start + 128 - margin) // 8 * 8
        pieces.append((first, end - first, start))
        first = end
    return pieces


def window_weights(line, cells, margin):
    block = line.block(cells)
    tables = []
    for first, count, start in windows(cells, margin):
        hi, lo = halves(block[first : first + count, start : start + 128])
        tables.append(np.block([[hi, hi], [lo, np.zeros_like(lo)]]))
    return np.concatenate(tables, axis=0)


def x_operator(hi, lo, w, margin):
    parts = []
    for first, count, start in windows(hi.shape[0], margin):
        cells = jnp.concatenate([hi[start : start + 128], lo[start : start + 128]], axis=0)
        r = dot(w[2 * first : 2 * (first + count)], cells)
        parts.append(r[:count] + r[count:])
    r = jnp.concatenate(parts, axis=0)
    return r[:, :128], r[:, 128:]


def sweep(planes, body, written):
    def step(i, carry):
        for j in range(0, span, 2):
            body(i * span + j)
            if (j + 2) % chunk == 0:
                for copy in written(i * (span // chunk) + j // chunk):
                    copy.start()
        return carry

    lax.fori_loop(0, planes // span, step, 0)
    for i in range(planes // chunk):
        for copy in written(i):
            copy.wait()


def local_kernel(f, wx, wy, dx_out, part_y, dx_low, dx_high, down, up, dx, sems):
    planes, n, cols = f.shape
    deriv, _ = line_operators()
    at = lax.broadcasted_iota(jnp.int32, (8, cols), 0)
    head, tail = powers_of(deriv.ratio, at, 3), powers_of(deriv.ratio, 7 - at, 3)
    inner = pl.ds(deriv_rim, n - 2 * deriv_rim)

    def written(i):
        part = pl.ds(i * chunk, chunk)
        return (pltpu.make_async_copy(dx.at[part, inner], dx_out.at[part, inner], sems.at[i]),)

    def body(p):
        hi, lo = split(jnp.concatenate([f[p], f[p + 1]], axis=-1))
        for j, r in enumerate(x_operator(hi, lo, wx, deriv_rim)):
            q = p + j
            at = slice(cols * j, cols * j + cols)
            part_y[q] = dot(jnp.concatenate([hi[:, at], lo[:, at]], axis=-1), wy[...])
            dx[q] = r
            dx_low[q] = r[:deriv_rim]
            dx_high[q] = r[n - deriv_rim :]
            row = pl.ds(q, 1)
            down[0, row, :] = geometric(f[q, : reach // 2, :], deriv.ratio, head, False)
            up[0, row, :] = geometric(f[q, n - reach // 2 :, :], deriv.ratio, tail, True)
            down[1, row, :] = f[q, 0:1, :]
            up[1, row, :] = f[q, n - 1 : n, :]

    sweep(planes, body, written)


def y_kernel(f, part_y, lower, upper, d_down, d_up, w, dy, gy, down, up, halo):
    planes, n, cols = f.shape
    _, smooth = line_operators()
    zero = jnp.zeros((planes, 128), F32)
    for c in range(0, n, 128):
        for k in range(16):
            rows = lower[k, :, c : c + 128] if k < 6 else upper[k - 6, :, c : c + 128] if k < 12 else zero
            halo[c // 128, pl.ds(k, planes, stride=16), :] = rows
    for k in range(2):
        down[5 + k] = d_down[k]
        up[5 + k] = d_up[k]
    at = lax.broadcasted_iota(jnp.int32, (8, cols), 0)
    head, tail = powers_of(smooth.ratio, at, 3), powers_of(smooth.ratio, 7 - at, 3)

    def step(i, carry):
        for j in range(span):
            q = i * span + j
            at = pl.ds(pl.multiple_of(q * 16, 16), 16)
            hi, lo = split(jnp.concatenate([halo[c, at, :] for c in range(n // 128)], axis=-1))
            faces = jnp.concatenate([hi, lo, hi], axis=0).T
            r = dot(jnp.concatenate([f[q].astype(BF16), faces], axis=-1), w[...]) + part_y[q]
            dy[q] = r[:, :128]
            g = r[:, 128:]
            gy[q] = g
            row = pl.ds(q, 1)
            down[0, row, :] = geometric(g[:reach], smooth.ratio, head, False)
            up[0, row, :] = geometric(g[n - reach :], smooth.ratio, tail, True)
            for k in range(4):
                down[1 + k, row, :] = g[k : k + 1]
                up[1 + k, row, :] = g[n - 4 + k : n - 3 + k]
        return carry

    lax.fori_loop(0, planes // span, step, 0)


def x_filter_kernel(gy, dy, w, dy_out, sm_out, sm_low, sm_high, sm, sems):
    planes, n, _ = gy.shape
    inner = pl.ds(filter_rim, n - 2 * filter_rim)

    def written(i):
        part = pl.ds(i * chunk, chunk)
        return (
            pltpu.make_async_copy(sm.at[part, inner], sm_out.at[part, inner], sems.at[0, i]),
            pltpu.make_async_copy(dy.at[part], dy_out.at[part], sems.at[1, i]),
        )

    def body(p):
        hi, lo = split(jnp.concatenate([gy[p], gy[p + 1]], axis=-1))
        for j, r in enumerate(x_operator(hi, lo, w, filter_rim)):
            sm[p + j] = r
            sm_low[p + j] = r[:filter_rim]
            sm_high[p + j] = r[n - filter_rim :]

    sweep(planes, body, written)


def rim_kernel(
    dx_low, dx_high, sm_low, sm_high, lower, upper, ds_low, ds_high, dc_low, dc_high, fs_low, fs_high, fc_low, fc_high,
    dx_in, sm_in, dx_out, sm_out, dl, dh, sl, sh, sems,
):
    planes = dx_low.shape[0]
    n = dx_out.shape[1]

    def written(i):
        part = pl.ds(i * group, group)
        return (
            pltpu.make_async_copy(dl.at[part], dx_out.at[part, pl.ds(0, deriv_rim)], sems.at[0, i]),
            pltpu.make_async_copy(dh.at[part], dx_out.at[part, pl.ds(n - deriv_rim, deriv_rim)], sems.at[1, i]),
            pltpu.make_async_copy(sl.at[part], sm_out.at[part, pl.ds(0, filter_rim)], sems.at[2, i]),
            pltpu.make_async_copy(sh.at[part], sm_out.at[part, pl.ds(n - filter_rim, filter_rim)], sems.at[3, i]),
        )

    def step(i, carry):
        for j in range(group):
            p = i * group + j
            row = pl.ds(p, 1)
            low = dx_low[p] + ds_low[...] * lower[5, row, :]
            high = dx_high[p] + ds_high[...] * upper[5, row, :]
            dl[p] = jnp.concatenate([low[:8] + dc_low[...] * lower[6, row, :], low[8:]], axis=0)
            dh[p] = jnp.concatenate([high[:-8], high[-8:] + dc_high[...] * upper[6, row, :]], axis=0)
            low = sm_low[p] + fs_low[...] * lower[0, row, :]
            high = sm_high[p] + fs_high[...] * upper[0, row, :]
            near_low, near_high = low[:8], high[-8:]
            for k in range(4):
                near_low = near_low + fc_low[k] * lower[1 + k, row, :]
                near_high = near_high + fc_high[k] * upper[1 + k, row, :]
            sl[p] = jnp.concatenate([near_low, low[8:]], axis=0)
            sh[p] = jnp.concatenate([high[:-8], near_high], axis=0)
        for copy in written(i):
            copy.start()
        return carry

    lax.fori_loop(0, planes // group, step, 0)
    for i in range(planes // group):
        for copy in written(i):
            copy.wait()


def tables(rows, cols):
    deriv, smooth = line_operators()
    t = {"wx_d": window_weights(deriv, rows, deriv_rim), "wx_f": window_weights(smooth, rows, filter_rim)}
    d_hi, d_lo = halves(deriv.block(cols).T)
    f_hi, f_lo = halves(smooth.block(cols).T)
    hi, lo = np.concatenate([d_hi, f_hi], axis=1), np.concatenate([d_lo, f_lo], axis=1)
    v = np.zeros((16, 2 * cols))
    low, high = smooth.from_below(cols), smooth.from_above(cols)
    v[0:5, cols:], v[6:11, cols:] = low.T, high.T
    low, high = deriv.from_below(cols), deriv.from_above(cols)
    v[5, :cols], v[4, :cols] = low[:, 0], low[:, 4]
    v[11, :cols], v[7, :cols] = high[:, 0], high[:, 1]
    v_hi, v_lo = halves(v)
    t["wy"] = np.concatenate([hi, hi], axis=0)
    t["wy_more"] = np.concatenate([lo, v_hi, v_hi, v_lo], axis=0)
    low, high = smooth.from_below(rows), smooth.from_above(rows)
    t["fs_low"], t["fs_high"] = lanes(low[:filter_rim, 0]), lanes(high[-filter_rim:, 0])
    t["fc_low"] = np.stack([lanes(low[:8, 1 + k]) for k in range(4)])
    t["fc_high"] = np.stack([lanes(high[-8:, 1 + k]) for k in range(4)])
    low, high = deriv.from_below(rows), deriv.from_above(rows)
    t["ds_low"], t["ds_high"] = lanes(low[:deriv_rim, 0]), lanes(high[-deriv_rim:, 0])
    t["dc_low"], t["dc_high"] = lanes(low[:8, 4]), lanes(high[-8:, 1])
    return {key: jnp.asarray(value) for key, value in t.items()}


def shifted(values, axis, by):
    count = lax.axis_size(axis)
    return lax.ppermute(values, axis, [(i, (i + by) % count) for i in range(count)])


def on_device(fields):
    shape = fields.shape
    rows, cols = shape[2:]
    planes = shape[0] * shape[1]
    block = (planes, rows, cols)
    t = tables(rows, cols)
    steps = planes // group
    y_face = (6, planes, rows)
    dx_rim, sm_rim = (planes, deriv_rim, cols), (planes, filter_rim, cols)
    f, y_down, y_up = call(
        "faces", face_kernel, [block, y_face, y_face],
        [pltpu.with_memory_space_constraint(fields.reshape(block), pltpu.HBM)], 10**9, 10**7,
        in_specs=[ANY], scratch=[pltpu.SemaphoreType.DMA((len(pieces),))],
    )
    y_lower = shifted(y_up, "gy", 1)
    y_upper = shifted(y_down, "gy", -1)
    few, face = (2, planes, cols), (7, planes, cols)
    copies = planes // chunk
    dx, part_y, dx_low, dx_high, d_down, d_up = call(
        "local", local_kernel, [block, (planes, rows, 2 * cols), dx_rim, dx_rim, few, few],
        [f, t["wx_d"], t["wy"]], 4 * 10**9, 10**7,
        out_specs=[ANY] + [VMEM] * 5, scratch=[pltpu.VMEM(block, F32), pltpu.SemaphoreType.DMA((copies,))],
    )
    dy, gy, x_down, x_up = call(
        "y_both", y_kernel, [block, block, face, face],
        [f, part_y, y_lower, y_upper, d_down, d_up, t["wy_more"]], 6 * 10**9, 2 * 10**7,
        scratch=[pltpu.VMEM((rows // 128, planes * 16, 128), F32)],
    )
    x_lower = shifted(x_up, "gx", 1)
    x_upper = shifted(x_down, "gx", -1)
    dy, sm, sm_low, sm_high = call(
        "x_filter", x_filter_kernel, [block, block, sm_rim, sm_rim], [gy, dy, t["wx_f"]], 4 * 10**9, 10**7,
        out_specs=[ANY, ANY, VMEM, VMEM],
        scratch=[pltpu.VMEM(block, F32), pltpu.SemaphoreType.DMA((2, copies))],
    )
    rims = ("ds_low", "ds_high", "dc_low", "dc_high", "fs_low", "fs_high", "fc_low", "fc_high")
    ins = [dx_low, dx_high, sm_low, sm_high, x_lower, x_upper] + [t[k] for k in rims]
    dx, sm = call(
        "rims", rim_kernel, [block, block], ins + [dx, sm], 10**8, 4 * 10**6,
        in_specs=[VMEM] * len(ins) + [ANY, ANY],
        out_specs=[ANY, ANY],
        scratch=[pltpu.VMEM(shape, F32) for shape in (dx_rim, dx_rim, sm_rim, sm_rim)]
        + [pltpu.SemaphoreType.DMA((4, steps))],
        aliases={len(ins): 0, len(ins) + 1: 1},
    )
    return tuple(out.reshape(shape) for out in (dx, dy, sm))


def solution(mesh):
    placed = P(None, None, "gx", "gy")
    return jax.shard_map(
        on_device, mesh=mesh, in_specs=(placed,), out_specs=(placed, placed, placed), check_vma=False
    )
```

time: 30.2 us -> 27.5 us (0.911)
  Pallas kernels: 19.6 us -> 14.8 us
  waiting for transfers between devices: 0.01 us -> 2.16 us
    pallas_call x5, Pallas kernels: 19.6 us -> 14.8 us  [call(): pl.pallas_call(kernel, in_specs=in_specs or [VMEM] * len(ins), out_specs=...]
    ppermute x4, waiting for transfers between devices: 0.01 us -> 2.16 us  [shifted(): lax.ppermute(values, axis, [(i, (i + by) % count) for i in range(count)])]
  transfers between devices with their start and end apart: 4 -> 4, of which waited for: 0 -> 1; matrix products, arithmetic and copies ran while one was open for 0% -> 0% of each run, Pallas kernels for 44% -> 28%
where the time goes in v3:
time: 27.5 us; the launch traced here: 27.3 us
  Pallas kernels  14.8 us (54%)
  starting transfers between devices  9.43 us (34%)
  waiting for transfers between devices  2.16 us (8%)
  between operations  0.82 us (3%)
    pallas_call x5, Pallas kernels, call(): pl.pallas_call(kernel, in_specs=in_specs or [VMEM] * len(ins), out_specs=...  14.8 us
    ppermute x4, starting transfers between devices, shifted(): lax.ppermute(values, axis, [(i, (i + by) % count) for i in range(count)])  9.43 us
    ppermute x4, waiting for transfers between devices, shifted(): lax.ppermute(values, axis, [(i, (i + by) % count) for i in range(count)])  2.16 us
  transfers between devices with their start and end apart: 4, of which 1 were waited for; matrix products, arithmetic and copies ran while one was open for 0% of the time, Pallas kernels for 28%

profile of v3, /device:TPU:0, one launch (start us, length us, event | category | flops | bytes accessed | tf_op | source)
XLA Modules:
  0.0 27.3 jit_solution(9723017480593828032)
XLA Ops:
  0.6 0.0 copy-start.10
  0.6 0.0 copy-start.9
  0.7 3.5 %faces.1 = (f32[40,256,128]{2,1,0:T(8,128)S(1)}, f32[6,40,256]{2,1,0:T(8,128)S(1)}, f32[6,40,256]{2,1,0:T(8,128)S(1)}) custom-call(f32[40,256,128]{2,1,0:T(8,128)} %bitcast.6), custom_call_target="tpu_custom_call" | custom-call | flops 1000000000 | bytes 10000000 | tf_op jit(solution)/shard_map/faces/pallas_call | solution.py:118
  4.1 1.6 %collective-permute-start = (f32[6,40,256]{2,1,0:T(8,128)S(1)}, f32[6,40,256]{2,1,0:T(8,128)S(1)}, u32[]{:S(2)}, u32[]{:S(2)}) collective-permute-start(f32[6,40,256]{2,1,0:T(8,128)S(1)} %get-tuple-element.26), channel_id=1, source_target_pairs={{0,1},{1,2},{2,3},{3,4},{4,5},{5,6},{6,7},{7,8},{8,9},{9,10},{10,1... | collective-permute-start | bytes 737288 | tf_op jit(solution)/shard_map/ppermute | solution.py:381
  5.8 4.8 %collective-permute-start.1 = (f32[6,40,256]{2,1,0:T(8,128)S(1)}, f32[6,40,256]{2,1,0:T(8,128)S(1)}, u32[]{:S(2)}, u32[]{:S(2)}) collective-permute-start(f32[6,40,256]{2,1,0:T(8,128)S(1)} %get-tuple-element.27), channel_id=1, source_target_pairs={{0,15},{1,0},{2,1},{3,2},{4,3},{5,4},{6,5},{7,6},{8,7},{9,8},{10,9... | collective-permute-start | bytes 737288 | tf_op jit(solution)/shard_map/ppermute | solution.py:381
  10.6 0.0 copy-done.9
  10.6 3.7 %local.1 = (f32[40,256,128]{2,1,0:T(8,128)}, f32[40,256,256]{2,1,0:T(8,128)S(1)}, f32[40,24,128]{2,1,0:T(8,128)S(1)}, f32[40,24,128]{2,1,0:T(8,128)S(1)}, f32[2,...) custom-call(f32[40,256,128]{2,1,0:T(8,128)S(1)} %get-tuple-element.22.f, bf16[512,256]{1,0:T(8,128)(2,1)S(1)} %copy-done.9, ...), custom_call_target="tpu_custom_call" | custom-call | flops 4000000000 | bytes 10000000 | tf_op jit(solution)/shard_map/local/pallas_call | solution.py:118
  14.3 2.1 %collective-permute-done.lower = f32[6,40,256]{2,1,0:T(8,128)S(1)} collective-permute-done((f32[6,40,256]{2,1,0:T(8,128)S(1)}, f32[6,40,256]{2,1,0:T(8,128)S(1)}, u32[]{:S(2)}, u32[]{:S(2)}) %collective-permute-start) | collective-permute-done | bytes 245792 | tf_op jit(solution)/shard_map/ppermute | solution.py:381
  16.5 0.0 collective-permute-done.1.upper
  16.5 2.0 %y_both.1 = (f32[40,256,128]{2,1,0:T(8,128)S(1)}, f32[40,256,128]{2,1,0:T(8,128)S(1)}, f32[7,40,128]{2,1,0:T(8,128)S(1)}, f32[7,40,128]{2,1,0:T(8,128)S(1)}) custom-call(f32[40,256,128]{2,1,0:T(8,128)S(1)} %get-tuple-element.22.f, f32[40,256,256]{2,1,0:T(8,128)S(1)} %get-tuple-element.25.part_y, f32[6,40,256]{2,1,0:T(8,128)S(1)} %collective-permute-done.lower, ...), custom_call_target="tpu_custom_call" | custom-call | flops 6000000000 | bytes 20000000 | tf_op jit(solution)/shard_map/y_both/pallas_call | solution.py:118
  18.5 0.0 collective-permute-start.2
  18.5 2.9 %collective-permute-start.3 = (f32[7,40,128]{2,1,0:T(8,128)S(1)}, f32[7,40,128]{2,1,0:T(8,128)S(1)}, u32[]{:S(2)}, u32[]{:S(2)}) collective-permute-start(f32[7,40,128]{2,1,0:T(8,128)S(1)} %get-tuple-element.35), channel_id=1, source_target_pairs={{0,112},{16,0},{32,16},{48,32},{64,48},{80,64},{96,80},{112,96},{1... | collective-permute-start | bytes 430088 | tf_op jit(solution)/shard_map/ppermute | solution.py:381
  21.5 0.0 copy-done.8
  21.5 0.0 copy-start.3
  21.5 0.0 copy-start.4
  21.5 0.0 copy-start.5
  21.5 0.0 copy-start.6
  21.5 0.0 copy-start.7
  21.5 3.9 %x_filter.1 = (f32[40,256,128]{2,1,0:T(8,128)}, f32[40,256,128]{2,1,0:T(8,128)}, f32[40,40,128]{2,1,0:T(8,128)S(1)}, f32[40,40,128]{2,1,0:T(8,128)S(1)}) custom-call(f32[40,256,128]{2,1,0:T(8,128)S(1)} %get-tuple-element.30.gy, f32[40,256,128]{2,1,0:T(8,128)S(1)} %get-tuple-element.31.dy, bf16[512,256]{1,0:T(8,128)(2,1)S(1)} %copy-done.8), custom_call_target="tpu_custom_call" | custom-call | flops 4000000000 | bytes 10000000 | tf_op jit(solution)/shard_map/x_filter/pallas_call | solution.py:118
  25.5 0.0 collective-permute-done.2.lower
  25.5 0.0 collective-permute-done.3.upper
  25.5 0.0 copy-done
  25.5 0.0 copy-done.1
  25.6 1.7 %rims.1 = (f32[40,256,128]{2,1,0:T(8,128)}, f32[40,256,128]{2,1,0:T(8,128)}) custom-call(f32[40,24,128]{2,1,0:T(8,128)S(1)} %get-tuple-element.23.dx_low, f32[40,24,128]{2,1,0:T(8,128)S(1)} %get-tuple-element.24.dx_high, f32[40,40,128]{2,1,0:T(8,128)S(1)} %get-tuple-element.32.sm_low, ...), custom_call_target="tpu_custom_call", output_to_operand_aliasing={{0}: (14, {}), {1}: (15, {})} | custom-call | flops 100000000 | bytes 4000000 | tf_op jit(solution)/shard_map/rims/pallas_call | solution.py:118
  (13 shorter events, 0.0 us)
Async XLA Ops:
  0.6 10.0 %copy-start.10 = (bf16[256,256]{1,0:T(8,128)(2,1)S(1)}, bf16[256,256]{1,0:T(8,128)(2,1)}, u32[]{:S(2)}) copy-start(bf16[256,256]{1,0:T(8,128)(2,1)} %constant.26.clone.wy) | copy-start | bytes 393220
  0.6 10.0 %copy-start.9 = (bf16[512,256]{1,0:T(8,128)(2,1)S(1)}, bf16[512,256]{1,0:T(8,128)(2,1)}, u32[]{:S(2)}) copy-start(bf16[512,256]{1,0:T(8,128)(2,1)} %constant.24.clone.wx) | copy-start | bytes 786436
  4.1 12.3 %collective-permute-start = (f32[6,40,256]{2,1,0:T(8,128)S(1)}, f32[6,40,256]{2,1,0:T(8,128)S(1)}, u32[]{:S(2)}, u32[]{:S(2)}) collective-permute-start(f32[6,40,256]{2,1,0:T(8,128)S(1)} %get-tuple-element.26), channel_id=1, source_target_pairs={{0,1},{1,2},{2,3},{3,4},{4,5},{5,6},{6,7},{7,8},{8,9},{9,10},{10,1... | collective-permute-start | bytes 737288 | tf_op jit(solution)/shard_map/ppermute | solution.py:381
  5.8 10.7 %collective-permute-start.1 = (f32[6,40,256]{2,1,0:T(8,128)S(1)}, f32[6,40,256]{2,1,0:T(8,128)S(1)}, u32[]{:S(2)}, u32[]{:S(2)}) collective-permute-start(f32[6,40,256]{2,1,0:T(8,128)S(1)} %get-tuple-element.27), channel_id=1, source_target_pairs={{0,15},{1,0},{2,1},{3,2},{4,3},{5,4},{6,5},{7,6},{8,7},{9,8},{10,9... | collective-permute-start | bytes 737288 | tf_op jit(solution)/shard_map/ppermute | solution.py:381
  10.6 5.9 %copy-start.11 = (bf16[176,256]{1,0:T(8,128)(2,1)S(1)}, bf16[176,256]{1,0:T(8,128)(2,1)}, u32[]{:S(2)}) copy-start(bf16[176,256]{1,0:T(8,128)(2,1)} %constant.27.clone.w) | copy-start | bytes 270340
  16.5 5.0 %copy-start.8 = (bf16[512,256]{1,0:T(8,128)(2,1)S(1)}, bf16[512,256]{1,0:T(8,128)(2,1)}, u32[]{:S(2)}) copy-start(bf16[512,256]{1,0:T(8,128)(2,1)} %constant.25.clone.w) | copy-start | bytes 786436
  18.5 7.0 %collective-permute-start.2 = (f32[7,40,128]{2,1,0:T(8,128)S(1)}, f32[7,40,128]{2,1,0:T(8,128)S(1)}, u32[]{:S(2)}, u32[]{:S(2)}) collective-permute-start(f32[7,40,128]{2,1,0:T(8,128)S(1)} %get-tuple-element.34), channel_id=1, source_target_pairs={{0,16},{16,32},{32,48},{48,64},{64,80},{80,96},{96,112},{112,0},{1... | collective-permute-start | bytes 430088 | tf_op jit(solution)/shard_map/ppermute | solution.py:381
  18.5 7.0 %collective-permute-start.3 = (f32[7,40,128]{2,1,0:T(8,128)S(1)}, f32[7,40,128]{2,1,0:T(8,128)S(1)}, u32[]{:S(2)}, u32[]{:S(2)}) collective-permute-start(f32[7,40,128]{2,1,0:T(8,128)S(1)} %get-tuple-element.35), channel_id=1, source_target_pairs={{0,112},{16,0},{32,16},{48,32},{64,48},{80,64},{96,80},{112,96},{1... | collective-permute-start | bytes 430088 | tf_op jit(solution)/shard_map/ppermute | solution.py:381
  21.5 4.0 %copy-start = (f32[40,128]{1,0:T(8,128)S(1)}, f32[40,128]{1,0:T(8,128)}, u32[]{:S(2)}) copy-start(f32[40,128]{1,0:T(8,128)} %constant.29.clone.fs_high) | copy-start | bytes 61444
  21.5 4.1 %copy-start.1 = (f32[40,128]{1,0:T(8,128)S(1)}, f32[40,128]{1,0:T(8,128)}, u32[]{:S(2)}) copy-start(f32[40,128]{1,0:T(8,128)} %constant.28.clone.fs_low) | copy-start | bytes 61444
  21.5 4.1 %copy-start.2 = (f32[4,8,128]{2,1,0:T(8,128)S(1)}, f32[4,8,128]{2,1,0:T(8,128)}, u32[]{:S(2)}) copy-start(f32[4,8,128]{2,1,0:T(8,128)} %constant.31.clone.fc_high) | copy-start | bytes 49156
  21.5 4.1 %copy-start.3 = (f32[4,8,128]{2,1,0:T(8,128)S(1)}, f32[4,8,128]{2,1,0:T(8,128)}, u32[]{:S(2)}) copy-start(f32[4,8,128]{2,1,0:T(8,128)} %constant.30.clone.fc_low) | copy-start | bytes 49156
  21.5 4.1 %copy-start.4 = (f32[24,128]{1,0:T(8,128)S(1)}, f32[24,128]{1,0:T(8,128)}, u32[]{:S(2)}) copy-start(f32[24,128]{1,0:T(8,128)} %constant.33.clone.ds_high) | copy-start | bytes 36868
  21.5 4.1 %copy-start.5 = (f32[24,128]{1,0:T(8,128)S(1)}, f32[24,128]{1,0:T(8,128)}, u32[]{:S(2)}) copy-start(f32[24,128]{1,0:T(8,128)} %constant.32.clone.ds_low) | copy-start | bytes 36868
  21.5 4.1 %copy-start.6 = (f32[8,128]{1,0:T(8,128)S(1)}, f32[8,128]{1,0:T(8,128)}, u32[]{:S(2)}) copy-start(f32[8,128]{1,0:T(8,128)} %constant.35.clone.dc_high) | copy-start | bytes 12292
  21.5 4.1 %copy-start.7 = (f32[8,128]{1,0:T(8,128)S(1)}, f32[8,128]{1,0:T(8,128)}, u32[]{:S(2)}) copy-start(f32[8,128]{1,0:T(8,128)} %constant.34.clone.dc_low) | copy-start | bytes 12292

commit v4 on v3

--- a/solution.py
+++ b/solution.py
@@ -18,10 +18,10 @@
 reach = 64
 filter_rim = 40
 deriv_rim = 24
-group = 8
 pieces = ((0, 8), (8, 8), (16, 8), (24, 8), (32, 8))
-span = 40
 chunk = 4
+lag = 8
+rim_chunk = 8
 
 
 def filter_weights():
@@ -209,104 +209,124 @@
     return r[:, :128], r[:, 128:]
 
 
-def sweep(planes, body, written):
-    def step(i, carry):
-        for j in range(0, span, 2):
-            body(i * span + j)
-            if (j + 2) % chunk == 0:
-                for copy in written(i * (span // chunk) + j // chunk):
-                    copy.start()
-        return carry
-
-    lax.fori_loop(0, planes // span, step, 0)
-    for i in range(planes // chunk):
-        for copy in written(i):
-            copy.wait()
-
-
-def local_kernel(f, wx, wy, dx_out, part_y, dx_low, dx_high, down, up, dx, sems):
+def sweep(planes, body, written, size=chunk):
+    started = []
+    for p in range(0, planes, 2):
+        body(p)
+        if (p + 2) % size == 0:
+            copies = written(p + 2 - size, size)
+            for copy in copies:
+                copy.start()
+            started += copies
+    for copy in started:
+        copy.wait()
+
+
+def dot3(rows, table):
+    n = table.shape[1] // 2
+    a, b = split(rows)
+    r = dot(a, table[...])
+    return r[:, :n] + r[:, n:] + dot(b, table[:, :n])
+
+
+def local_kernel(f, wx, wy, by, dx_out, part_y, dx_low, dx_high, down, up, own, dx, sems):
     planes, n, cols = f.shape
-    deriv, _ = line_operators()
+    deriv, smooth = line_operators()
     at = lax.broadcasted_iota(jnp.int32, (8, cols), 0)
-    head, tail = powers_of(deriv.ratio, at, 3), powers_of(deriv.ratio, 7 - at, 3)
+    d_head, d_tail = powers_of(deriv.ratio, at, 3), powers_of(deriv.ratio, 7 - at, 3)
+    f_head, f_tail = powers_of(smooth.ratio, at, 3), powers_of(smooth.ratio, 7 - at, 3)
     inner = pl.ds(deriv_rim, n - 2 * deriv_rim)
 
-    def written(i):
-        part = pl.ds(i * chunk, chunk)
-        return (pltpu.make_async_copy(dx.at[part, inner], dx_out.at[part, inner], sems.at[i]),)
+    def written(first, count):
+        part = pl.ds(first, count)
+        return [pltpu.make_async_copy(dx.at[part, inner], dx_out.at[part, inner], sems.at[first // chunk])]
 
     def body(p):
         hi, lo = split(jnp.concatenate([f[p], f[p + 1]], axis=-1))
+        for j in range(2):
+            at = slice(cols * j, cols * j + cols)
+            part_y[p + j] = dot(jnp.concatenate([hi[:, at], lo[:, at]], axis=-1), wy[...])
         for j, r in enumerate(x_operator(hi, lo, wx, deriv_rim)):
             q = p + j
-            at = slice(cols * j, cols * j + cols)
-            part_y[q] = dot(jnp.concatenate([hi[:, at], lo[:, at]], axis=-1), wy[...])
             dx[q] = r
             dx_low[q] = r[:deriv_rim]
             dx_high[q] = r[n - deriv_rim :]
-            row = pl.ds(q, 1)
-            down[0, row, :] = geometric(f[q, : reach // 2, :], deriv.ratio, head, False)
-            up[0, row, :] = geometric(f[q, n - reach // 2 :, :], deriv.ratio, tail, True)
-            down[1, row, :] = f[q, 0:1, :]
-            up[1, row, :] = f[q, n - 1 : n, :]
+            row = slice(q, q + 1)
+            down[0, row, :] = geometric(f[q, :reach, :], smooth.ratio, f_head, False)
+            up[0, row, :] = geometric(f[q, n - reach :, :], smooth.ratio, f_tail, True)
+            down[5, row, :] = geometric(f[q, : reach // 2, :], deriv.ratio, d_head, False)
+            up[5, row, :] = geometric(f[q, n - reach // 2 :, :], deriv.ratio, d_tail, True)
+            for k in range(4):
+                down[1 + k, row, :] = f[q, k : k + 1, :]
+                up[1 + k, row, :] = f[q, n - 4 + k : n - 3 + k, :]
 
     sweep(planes, body, written)
-
-
-def y_kernel(f, part_y, lower, upper, d_down, d_up, w, dy, gy, down, up, halo):
+    rows = jnp.concatenate([down[k] for k in range(5)] + [up[k] for k in range(5)], axis=0)
+    own[...] = dot3(rows, by[...])
+
+
+def x_face_kernel(own, x_down, x_up, lower, upper, tx, vy, down, up):
+    planes = lower.shape[1]
+    rows = jnp.concatenate([lower[g] for g in range(5)] + [upper[g] for g in range(5)], axis=0)
+    r = dot3(rows, tx[...])
+    z = r[:planes]
+    for g in range(1, 10):
+        z = z + pltpu.roll(r[g * planes : (g + 1) * planes], 10 * g, 1)
+    rows = jnp.concatenate([z] + [pltpu.roll(z, 128 - k, 1) for k in range(1, 10)], axis=0)
+    total = own[...] + dot3(rows, vy[...])
+    for k in range(5):
+        down[k] = total[k * planes : (k + 1) * planes]
+        up[k] = total[(5 + k) * planes : (6 + k) * planes]
+    down[5] = x_down[5]
+    up[5] = x_up[5]
+    down[6] = x_down[1]
+    up[6] = x_up[4]
+
+
+def late_kernel(f, part_y, lower, upper, wy, wx, dy_out, sm_out, sm_low, sm_high, halo, dy, gy, sm, sems):
     planes, n, cols = f.shape
-    _, smooth = line_operators()
     zero = jnp.zeros((planes, 128), F32)
     for c in range(0, n, 128):
         for k in range(16):
             rows = lower[k, :, c : c + 128] if k < 6 else upper[k - 6, :, c : c + 128] if k < 12 else zero
             halo[c // 128, pl.ds(k, planes, stride=16), :] = rows
-    for k in range(2):
-        down[5 + k] = d_down[k]
-        up[5 + k] = d_up[k]
-    at = lax.broadcasted_iota(jnp.int32, (8, cols), 0)
-    head, tail = powers_of(smooth.ratio, at, 3), powers_of(smooth.ratio, 7 - at, 3)
-
-    def step(i, carry):
-        for j in range(span):
-            q = i * span + j
-            at = pl.ds(pl.multiple_of(q * 16, 16), 16)
+    inner = pl.ds(filter_rim, n - 2 * filter_rim)
+
+    started = []
+
+    def send(source, target, number):
+        started.append(pltpu.make_async_copy(source, target, number))
+        started[-1].start()
+
+    def y_rows(p):
+        for q in (p, p + 1):
+            at = slice(16 * q, 16 * q + 16)
             hi, lo = split(jnp.concatenate([halo[c, at, :] for c in range(n // 128)], axis=-1))
             faces = jnp.concatenate([hi, lo, hi], axis=0).T
-            r = dot(jnp.concatenate([f[q].astype(BF16), faces], axis=-1), w[...]) + part_y[q]
-            dy[q] = r[:, :128]
-            g = r[:, 128:]
-            gy[q] = g
-            row = pl.ds(q, 1)
-            down[0, row, :] = geometric(g[:reach], smooth.ratio, head, False)
-            up[0, row, :] = geometric(g[n - reach :], smooth.ratio, tail, True)
-            for k in range(4):
-                down[1 + k, row, :] = g[k : k + 1]
-                up[1 + k, row, :] = g[n - 4 + k : n - 3 + k]
-        return carry
-
-    lax.fori_loop(0, planes // span, step, 0)
-
-
-def x_filter_kernel(gy, dy, w, dy_out, sm_out, sm_low, sm_high, sm, sems):
-    planes, n, _ = gy.shape
-    inner = pl.ds(filter_rim, n - 2 * filter_rim)
-
-    def written(i):
-        part = pl.ds(i * chunk, chunk)
-        return (
-            pltpu.make_async_copy(sm.at[part, inner], sm_out.at[part, inner], sems.at[0, i]),
-            pltpu.make_async_copy(dy.at[part], dy_out.at[part], sems.at[1, i]),
-        )
-
-    def body(p):
+            r = dot(jnp.concatenate([f[q].astype(BF16), faces], axis=-1), wy[...]) + part_y[q]
+            dy[q] = r[:, :cols]
+            gy[q] = r[:, cols:]
+
+    def x_rows(p):
         hi, lo = split(jnp.concatenate([gy[p], gy[p + 1]], axis=-1))
-        for j, r in enumerate(x_operator(hi, lo, w, filter_rim)):
+        for j, r in enumerate(x_operator(hi, lo, wx, filter_rim)):
             sm[p + j] = r
             sm_low[p + j] = r[:filter_rim]
             sm_high[p + j] = r[n - filter_rim :]
 
-    sweep(planes, body, written)
+    for p in range(0, planes + lag, 2):
+        if p < planes:
+            y_rows(p)
+        if p >= lag:
+            x_rows(p - lag)
+        if p < planes and (p + 2) % chunk == 0:
+            part = pl.ds(p + 2 - chunk, chunk)
+            send(dy.at[part], dy_out.at[part], sems.at[0, p // chunk])
+        if p >= lag and (p - lag + 2) % chunk == 0:
+            part = pl.ds(p - lag + 2 - chunk, chunk)
+            send(sm.at[part, inner], sm_out.at[part, inner], sems.at[1, (p - lag) // chunk])
+    for copy in started:
+        copy.wait()
 
 
 def rim_kernel(
@@ -316,19 +336,18 @@
     planes = dx_low.shape[0]
     n = dx_out.shape[1]
 
-    def written(i):
-        part = pl.ds(i * group, group)
-        return (
-            pltpu.make_async_copy(dl.at[part], dx_out.at[part, pl.ds(0, deriv_rim)], sems.at[0, i]),
-            pltpu.make_async_copy(dh.at[part], dx_out.at[part, pl.ds(n - deriv_rim, deriv_rim)], sems.at[1, i]),
-            pltpu.make_async_copy(sl.at[part], sm_out.at[part, pl.ds(0, filter_rim)], sems.at[2, i]),
-            pltpu.make_async_copy(sh.at[part], sm_out.at[part, pl.ds(n - filter_rim, filter_rim)], sems.at[3, i]),
-        )
-
-    def step(i, carry):
-        for j in range(group):
-            p = i * group + j
-            row = pl.ds(p, 1)
+    def written(first, count):
+        part, number = pl.ds(first, count), first // rim_chunk
+        return [
+            pltpu.make_async_copy(sl.at[part], sm_out.at[part, pl.ds(0, filter_rim)], sems.at[0, number]),
+            pltpu.make_async_copy(sh.at[part], sm_out.at[part, pl.ds(n - filter_rim, filter_rim)], sems.at[1, number]),
+            pltpu.make_async_copy(dl.at[part], dx_out.at[part, pl.ds(0, deriv_rim)], sems.at[2, number]),
+            pltpu.make_async_copy(dh.at[part], dx_out.at[part, pl.ds(n - deriv_rim, deriv_rim)], sems.at[3, number]),
+        ]
+
+    def body(q):
+        for p in (q, q + 1):
+            row = slice(p, p + 1)
             low = dx_low[p] + ds_low[...] * lower[5, row, :]
             high = dx_high[p] + ds_high[...] * upper[5, row, :]
             dl[p] = jnp.concatenate([low[:8] + dc_low[...] * lower[6, row, :], low[8:]], axis=0)
@@ -341,14 +360,8 @@
                 near_high = near_high + fc_high[k] * upper[1 + k, row, :]
             sl[p] = jnp.concatenate([near_low, low[8:]], axis=0)
             sh[p] = jnp.concatenate([high[:-8], near_high], axis=0)
-        for copy in written(i):
-            copy.start()
-        return carry
-
-    lax.fori_loop(0, planes // group, step, 0)
-    for i in range(planes // group):
-        for copy in written(i):
-            copy.wait()
+
+    sweep(planes, body, written, rim_chunk)
 
 
 def tables(rows, cols):
@@ -366,6 +379,24 @@
     v_hi, v_lo = halves(v)
     t["wy"] = np.concatenate([hi, hi], axis=0)
     t["wy_more"] = np.concatenate([lo, v_hi, v_hi, v_lo], axis=0)
+    powers = lambda line, count: line.ratio ** np.arange(count)
+    hi, lo = halves(smooth.block(cols).T)
+    t["by"] = np.concatenate([hi, lo], axis=1)
+    tx = np.zeros((rows, 128))
+    tx[:, 0] = powers(smooth, rows)
+    tx[:, 5] = tx[::-1, 0]
+    for k in range(4):
+        tx[k, 1 + k] = 1.0
+        tx[rows - 4 + k, 6 + k] = 1.0
+    hi, lo = halves(tx)
+    t["tx"] = np.concatenate([hi, lo], axis=1)
+    low, high = smooth.from_below(cols), smooth.from_above(cols)
+    vy = np.zeros((128, cols))
+    for g in range(5):
+        vy[10 * g] = low[:, g]
+        vy[10 * (5 + g)] = high[:, g]
+    hi, lo = halves(vy)
+    t["vy"] = np.concatenate([hi, lo], axis=1)
     low, high = smooth.from_below(rows), smooth.from_above(rows)
     t["fs_low"], t["fs_high"] = lanes(low[:filter_rim, 0]), lanes(high[-filter_rim:, 0])
     t["fc_low"] = np.stack([lanes(low[:8, 1 + k]) for k in range(4)])
@@ -387,7 +418,6 @@
     planes = shape[0] * shape[1]
     block = (planes, rows, cols)
     t = tables(rows, cols)
-    steps = planes // group
     y_face = (6, planes, rows)
     dx_rim, sm_rim = (planes, deriv_rim, cols), (planes, filter_rim, cols)
     f, y_down, y_up = call(
@@ -397,24 +427,31 @@
     )
     y_lower = shifted(y_up, "gy", 1)
     y_upper = shifted(y_down, "gy", -1)
-    few, face = (2, planes, cols), (7, planes, cols)
+    face = (7, planes, cols)
     copies = planes // chunk
-    dx, part_y, dx_low, dx_high, d_down, d_up = call(
-        "local", local_kernel, [block, (planes, rows, 2 * cols), dx_rim, dx_rim, few, few],
-        [f, t["wx_d"], t["wy"]], 4 * 10**9, 10**7,
-        out_specs=[ANY] + [VMEM] * 5, scratch=[pltpu.VMEM(block, F32), pltpu.SemaphoreType.DMA((copies,))],
-    )
-    dy, gy, x_down, x_up = call(
-        "y_both", y_kernel, [block, block, face, face],
-        [f, part_y, y_lower, y_upper, d_down, d_up, t["wy_more"]], 6 * 10**9, 2 * 10**7,
-        scratch=[pltpu.VMEM((rows // 128, planes * 16, 128), F32)],
+    dx, part_y, dx_low, dx_high, x_down, x_up, own = call(
+        "local", local_kernel,
+        [block, (planes, rows, 2 * cols), dx_rim, dx_rim, (6, planes, cols), (6, planes, cols), (10 * planes, cols)],
+        [f, t["wx_d"], t["wy"], t["by"]], 4 * 10**9, 10**7,
+        out_specs=[ANY] + [VMEM] * 6, scratch=[pltpu.VMEM(block, F32), pltpu.SemaphoreType.DMA((copies,))],
+    )
+    x_down, x_up = call(
+        "x_faces", x_face_kernel, [face, face], [own, x_down, x_up, y_lower, y_upper, t["tx"], t["vy"]], 10**8, 10**6
     )
     x_lower = shifted(x_up, "gx", 1)
     x_upper = shifted(x_down, "gx", -1)
     dy, sm, sm_low, sm_high = call(
-        "x_filter", x_filter_kernel, [block, block, sm_rim, sm_rim], [gy, dy, t["wx_f"]], 4 * 10**9, 10**7,
+        "late", late_kernel, [block, block, sm_rim, sm_rim],
+        [f, part_y, y_lower, y_upper, t["wy_more"], t["wx_f"]], 6 * 10**9, 2 * 10**7,
         out_specs=[ANY, ANY, VMEM, VMEM],
-        scratch=[pltpu.VMEM(block, F32), pltpu.SemaphoreType.DMA((2, copies))],
+        scratch=[
+            pltpu.VMEM((rows // 128, planes * 16, 128), F32),
+            pltpu.VMEM(block, F32),
+            pltpu.VMEM(block, F32),
+            pltpu.VMEM(block, F32),
+            pltpu.SemaphoreType.DMA((2, copies)),
+        ],
+        limit=24,
     )
     rims = ("ds_low", "ds_high", "dc_low", "dc_high", "fs_low", "fs_high", "fc_low", "fc_high")
     ins = [dx_low, dx_high, sm_low, sm_high, x_lower, x_upper] + [t[k] for k in rims]
@@ -423,7 +460,7 @@
         in_specs=[VMEM] * len(ins) + [ANY, ANY],
         out_specs=[ANY, ANY],
         scratch=[pltpu.VMEM(shape, F32) for shape in (dx_rim, dx_rim, sm_rim, sm_rim)]
-        + [pltpu.SemaphoreType.DMA((4, steps))],
+        + [pltpu.SemaphoreType.DMA((4, planes // rim_chunk))],
         aliases={len(ins): 0, len(ins) + 1: 1},
     )
     return tuple(out.reshape(shape) for out in (dx, dy, sm))

time: 27.5 us -> 26.7 us (0.971)
  waiting for transfers between devices: 2.16 us -> 1.71 us
  Pallas kernels: 14.8 us -> 14.5 us
    ppermute x4, waiting for transfers between devices: 2.16 us -> 1.71 us  [shifted(): lax.ppermute(values, axis, [(i, (i + by) % count) for i in range(count)])]
    pallas_call x5, Pallas kernels: 14.8 us -> 14.5 us  [call(): pl.pallas_call(kernel, in_specs=in_specs or [VMEM] * len(ins), out_specs=...]
  transfers between devices with their start and end apart: 4 -> 4, of which waited for: 1 -> 1; matrix products, arithmetic and copies ran while one was open for 0% -> 0% of each run, Pallas kernels for 28% -> 33%
where the time goes in v4:
time: 26.7 us; the launch traced here: 26.6 us
  Pallas kernels  14.5 us (54%)
  starting transfers between devices  9.43 us (35%)
  waiting for transfers between devices  1.71 us (6%)
  between operations  0.86 us (3%)
    pallas_call x5, Pallas kernels, call(): pl.pallas_call(kernel, in_specs=in_specs or [VMEM] * len(ins), out_specs=...  14.5 us
    ppermute x4, starting transfers between devices, shifted(): lax.ppermute(values, axis, [(i, (i + by) % count) for i in range(count)])  9.43 us
    ppermute x4, waiting for transfers between devices, shifted(): lax.ppermute(values, axis, [(i, (i + by) % count) for i in range(count)])  1.71 us
  transfers between devices with their start and end apart: 4, of which 1 were waited for; matrix products, arithmetic and copies ran while one was open for 0% of the time, Pallas kernels for 33%

profile of v4, /device:TPU:0, one launch (start us, length us, event | category | flops | bytes accessed | tf_op | source)
XLA Modules:
  0.0 26.6 jit_solution(15081962825558688714)
XLA Ops:
  0.6 0.0 copy-start.14
  0.6 0.0 copy-start.12
  0.7 0.0 copy-start.11
  0.7 3.5 %faces.1 = (f32[40,256,128]{2,1,0:T(8,128)S(1)}, f32[6,40,256]{2,1,0:T(8,128)S(1)}, f32[6,40,256]{2,1,0:T(8,128)S(1)}) custom-call(f32[40,256,128]{2,1,0:T(8,128)} %bitcast.6), custom_call_target="tpu_custom_call" | custom-call | flops 1000000000 | bytes 10000000 | tf_op jit(solution)/shard_map/faces/pallas_call | solution.py:118
  4.1 1.6 %collective-permute-start = (f32[6,40,256]{2,1,0:T(8,128)S(1)}, f32[6,40,256]{2,1,0:T(8,128)S(1)}, u32[]{:S(2)}, u32[]{:S(2)}) collective-permute-start(f32[6,40,256]{2,1,0:T(8,128)S(1)} %get-tuple-element.25), channel_id=1, source_target_pairs={{0,1},{1,2},{2,3},{3,4},{4,5},{5,6},{6,7},{7,8},{8,9},{9,10},{10,1... | collective-permute-start | bytes 737288 | tf_op jit(solution)/shard_map/ppermute | solution.py:412
  5.8 4.8 %collective-permute-start.1 = (f32[6,40,256]{2,1,0:T(8,128)S(1)}, f32[6,40,256]{2,1,0:T(8,128)S(1)}, u32[]{:S(2)}, u32[]{:S(2)}) collective-permute-start(f32[6,40,256]{2,1,0:T(8,128)S(1)} %get-tuple-element.26), channel_id=1, source_target_pairs={{0,15},{1,0},{2,1},{3,2},{4,3},{5,4},{6,5},{7,6},{8,7},{9,8},{10,9... | collective-permute-start | bytes 737288 | tf_op jit(solution)/shard_map/ppermute | solution.py:412
  10.6 0.0 copy-start.1
  10.6 0.0 copy-start.10
  10.7 0.0 copy-start.13
  10.7 4.1 %local.1 = (f32[40,256,128]{2,1,0:T(8,128)}, f32[40,256,256]{2,1,0:T(8,128)S(1)}, f32[40,24,128]{2,1,0:T(8,128)S(1)}, f32[40,24,128]{2,1,0:T(8,128)S(1)}, f32[6,...) custom-call(f32[40,256,128]{2,1,0:T(8,128)S(1)} %get-tuple-element.21.f, ...), custom_call_target="tpu_custom_call" | custom-call | flops 4000000000 | bytes 10000000 | tf_op jit(solution)/shard_map/local/pallas_call | solution.py:118
  14.8 1.7 %collective-permute-done.lower = f32[6,40,256]{2,1,0:T(8,128)S(1)} collective-permute-done((f32[6,40,256]{2,1,0:T(8,128)S(1)}, f32[6,40,256]{2,1,0:T(8,128)S(1)}, u32[]{:S(2)}, u32[]{:S(2)}) %collective-permute-start) | collective-permute-done | bytes 245792 | tf_op jit(solution)/shard_map/ppermute | solution.py:412
  16.5 0.0 collective-permute-done.1.upper
  16.5 0.6 %x_faces.1 = (f32[7,40,128]{2,1,0:T(8,128)S(1)}, f32[7,40,128]{2,1,0:T(8,128)S(1)}) custom-call(f32[400,128]{1,0:T(8,128)S(1)} %get-tuple-element.29.own, f32[6,40,128]{2,1,0:T(8,128)S(1)} %get-tuple-element.30.x_down, f32[6,40,128]{2,1,0:T(8,128)S(1)} %get-tuple-element.31.x_up, f32[6,40,256]{2,1,0:T(8,128)S(1)} %collective-permute-done.lower, ...), custom_call_target="tpu_custom_call" | custom-call | flops 100000000 | bytes 1000000 | tf_op jit(solution)/shard_map/x_faces/pallas_call | solution.py:118
  17.1 0.0 collective-permute-start.2
  17.2 2.9 %collective-permute-start.3 = (f32[7,40,128]{2,1,0:T(8,128)S(1)}, f32[7,40,128]{2,1,0:T(8,128)S(1)}, u32[]{:S(2)}, u32[]{:S(2)}) collective-permute-start(f32[7,40,128]{2,1,0:T(8,128)S(1)} %get-tuple-element.33), channel_id=1, source_target_pairs={{0,112},{16,0},{32,16},{48,32},{64,48},{80,64},{96,80},{112,96},{1... | collective-permute-start | bytes 430088 | tf_op jit(solution)/shard_map/ppermute | solution.py:412
  20.1 0.0 copy-start.4
  20.1 0.0 copy-start.5
  20.2 0.0 copy-start.6
  20.2 0.0 copy-start.7
  20.2 0.0 copy-start.8
  20.2 0.0 copy-start.9
  20.2 4.6 %late.1 = (f32[40,256,128]{2,1,0:T(8,128)}, f32[40,256,128]{2,1,0:T(8,128)}, f32[40,40,128]{2,1,0:T(8,128)S(1)}, f32[40,40,128]{2,1,0:T(8,128)S(1)}) custom-call(f32[40,256,128]{2,1,0:T(8,128)S(1)} %get-tuple-element.21.f, f32[40,256,256]{2,1,0:T(8,128)S(1)} %get-tuple-element.24.part_y, f32[6,40,256]{2,1,0:T(8,128)S(1)} %collective-permute-done.lower, ...), custom_call_target="tpu_custom_call" | custom-call | flops 6000000000 | bytes 20000000 | tf_op jit(solution)/shard_map/late/pallas_call | solution.py:118
  24.8 0.0 collective-permute-done.3.upper
  24.9 1.7 %rims.1 = (f32[40,256,128]{2,1,0:T(8,128)}, f32[40,256,128]{2,1,0:T(8,128)}) custom-call(f32[40,24,128]{2,1,0:T(8,128)S(1)} %get-tuple-element.22.dx_low, f32[40,24,128]{2,1,0:T(8,128)S(1)} %get-tuple-element.23.dx_high, f32[40,40,128]{2,1,0:T(8,128)S(1)} %get-tuple-element.27.sm_low, ...), custom_call_target="tpu_custom_call", output_to_operand_aliasing={{0}: (14, {}), {1}: (15, {})} | custom-call | flops 100000000 | bytes 4000000 | tf_op jit(solution)/shard_map/rims/pallas_call | solution.py:118
  (19 shorter events, 0.0 us)
Async XLA Ops:
  0.6 10.0 %copy-start.14 = (bf16[128,256]{1,0:T(8,128)(2,1)S(1)}, bf16[128,256]{1,0:T(8,128)(2,1)}, u32[]{:S(2)}) copy-start(bf16[128,256]{1,0:T(8,128)(2,1)} %constant.34.clone.by) | copy-start | bytes 196612
  0.6 10.0 %copy-start.12 = (bf16[256,256]{1,0:T(8,128)(2,1)S(1)}, bf16[256,256]{1,0:T(8,128)(2,1)}, u32[]{:S(2)}) copy-start(bf16[256,256]{1,0:T(8,128)(2,1)} %constant.32.clone.wy) | copy-start | bytes 393220
  0.7 10.0 %copy-start.11 = (bf16[512,256]{1,0:T(8,128)(2,1)S(1)}, bf16[512,256]{1,0:T(8,128)(2,1)}, u32[]{:S(2)}) copy-start(bf16[512,256]{1,0:T(8,128)(2,1)} %constant.30.clone.wx) | copy-start | bytes 786436
  4.1 12.3 %collective-permute-start = (f32[6,40,256]{2,1,0:T(8,128)S(1)}, f32[6,40,256]{2,1,0:T(8,128)S(1)}, u32[]{:S(2)}, u32[]{:S(2)}) collective-permute-start(f32[6,40,256]{2,1,0:T(8,128)S(1)} %get-tuple-element.25), channel_id=1, source_target_pairs={{0,1},{1,2},{2,3},{3,4},{4,5},{5,6},{6,7},{7,8},{8,9},{9,10},{10,1... | collective-permute-start | bytes 737288 | tf_op jit(solution)/shard_map/ppermute | solution.py:412
  5.8 10.7 %collective-permute-start.1 = (f32[6,40,256]{2,1,0:T(8,128)S(1)}, f32[6,40,256]{2,1,0:T(8,128)S(1)}, u32[]{:S(2)}, u32[]{:S(2)}) collective-permute-start(f32[6,40,256]{2,1,0:T(8,128)S(1)} %get-tuple-element.26), channel_id=1, source_target_pairs={{0,15},{1,0},{2,1},{3,2},{4,3},{5,4},{6,5},{7,6},{8,7},{9,8},{10,9... | collective-permute-start | bytes 737288 | tf_op jit(solution)/shard_map/ppermute | solution.py:412
  10.6 5.9 %copy-start = (bf16[256,256]{1,0:T(8,128)(2,1)S(1)}, bf16[256,256]{1,0:T(8,128)(2,1)}, u32[]{:S(2)}) copy-start(bf16[256,256]{1,0:T(8,128)(2,1)} %constant.35.clone.tx) | copy-start | bytes 393220
  10.6 5.9 %copy-start.1 = (bf16[128,256]{1,0:T(8,128)(2,1)S(1)}, bf16[128,256]{1,0:T(8,128)(2,1)}, u32[]{:S(2)}) copy-start(bf16[128,256]{1,0:T(8,128)(2,1)} %constant.36.clone.vy) | copy-start | bytes 196612
  10.6 9.5 %copy-start.10 = (bf16[512,256]{1,0:T(8,128)(2,1)S(1)}, bf16[512,256]{1,0:T(8,128)(2,1)}, u32[]{:S(2)}) copy-start(bf16[512,256]{1,0:T(8,128)(2,1)} %constant.31.clone.wx) | copy-start | bytes 786436
  10.7 9.5 %copy-start.13 = (bf16[176,256]{1,0:T(8,128)(2,1)S(1)}, bf16[176,256]{1,0:T(8,128)(2,1)}, u32[]{:S(2)}) copy-start(bf16[176,256]{1,0:T(8,128)(2,1)} %constant.33.clone.wy) | copy-start | bytes 270340
  17.1 7.6 %collective-permute-start.2 = (f32[7,40,128]{2,1,0:T(8,128)S(1)}, f32[7,40,128]{2,1,0:T(8,128)S(1)}, u32[]{:S(2)}, u32[]{:S(2)}) collective-permute-start(f32[7,40,128]{2,1,0:T(8,128)S(1)} %get-tuple-element.32), channel_id=1, source_target_pairs={{0,16},{16,32},{32,48},{48,64},{64,80},{80,96},{96,112},{112,0},{1... | collective-permute-start | bytes 430088 | tf_op jit(solution)/shard_map/ppermute | solution.py:412
  17.2 7.6 %collective-permute-start.3 = (f32[7,40,128]{2,1,0:T(8,128)S(1)}, f32[7,40,128]{2,1,0:T(8,128)S(1)}, u32[]{:S(2)}, u32[]{:S(2)}) collective-permute-start(f32[7,40,128]{2,1,0:T(8,128)S(1)} %get-tuple-element.33), channel_id=1, source_target_pairs={{0,112},{16,0},{32,16},{48,32},{64,48},{80,64},{96,80},{112,96},{1... | collective-permute-start | bytes 430088 | tf_op jit(solution)/shard_map/ppermute | solution.py:412
  20.1 4.7 %copy-start.2 = (f32[40,128]{1,0:T(8,128)S(1)}, f32[40,128]{1,0:T(8,128)}, u32[]{:S(2)}) copy-start(f32[40,128]{1,0:T(8,128)} %constant.38.clone.fs_high) | copy-start | bytes 61444
  20.1 4.7 %copy-start.3 = (f32[40,128]{1,0:T(8,128)S(1)}, f32[40,128]{1,0:T(8,128)}, u32[]{:S(2)}) copy-start(f32[40,128]{1,0:T(8,128)} %constant.37.clone.fs_low) | copy-start | bytes 61444
  20.1 4.7 %copy-start.4 = (f32[4,8,128]{2,1,0:T(8,128)S(1)}, f32[4,8,128]{2,1,0:T(8,128)}, u32[]{:S(2)}) copy-start(f32[4,8,128]{2,1,0:T(8,128)} %constant.40.clone.fc_high) | copy-start | bytes 49156
  20.1 4.7 %copy-start.5 = (f32[4,8,128]{2,1,0:T(8,128)S(1)}, f32[4,8,128]{2,1,0:T(8,128)}, u32[]{:S(2)}) copy-start(f32[4,8,128]{2,1,0:T(8,128)} %constant.39.clone.fc_low) | copy-start | bytes 49156
  20.2 4.7 %copy-start.6 = (f32[24,128]{1,0:T(8,128)S(1)}, f32[24,128]{1,0:T(8,128)}, u32[]{:S(2)}) copy-start(f32[24,128]{1,0:T(8,128)} %constant.42.clone.ds_high) | copy-start | bytes 36868
  20.2 4.7 %copy-start.7 = (f32[24,128]{1,0:T(8,128)S(1)}, f32[24,128]{1,0:T(8,128)}, u32[]{:S(2)}) copy-start(f32[24,128]{1,0:T(8,128)} %constant.41.clone.ds_low) | copy-start | bytes 36868
  20.2 4.7 %copy-start.8 = (f32[8,128]{1,0:T(8,128)S(1)}, f32[8,128]{1,0:T(8,128)}, u32[]{:S(2)}) copy-start(f32[8,128]{1,0:T(8,128)} %constant.44.clone.dc_high) | copy-start | bytes 12292
  20.2 4.7 %copy-start.9 = (f32[8,128]{1,0:T(8,128)S(1)}, f32[8,128]{1,0:T(8,128)}, u32[]{:S(2)}) copy-start(f32[8,128]{1,0:T(8,128)} %constant.43.clone.dc_low) | copy-start | bytes 12292

commit v5 on v4

--- a/solution.py
+++ b/solution.py
@@ -21,6 +21,7 @@
 pieces = ((0, 8), (8, 8), (16, 8), (24, 8), (32, 8))
 chunk = 4
 lag = 8
+ahead = 16
 rim_chunk = 8
 
 
@@ -229,7 +230,7 @@
     return r[:, :n] + r[:, n:] + dot(b, table[:, :n])
 
 
-def local_kernel(f, wx, wy, by, dx_out, part_y, dx_low, dx_high, down, up, own, dx, sems):
+def local_kernel(f, wx, wy, wy_more, wx_f, by, dx_out, part_y, dx_low, dx_high, down, up, own, dx, sems):
     planes, n, cols = f.shape
     deriv, smooth = line_operators()
     at = lax.broadcasted_iota(jnp.int32, (8, cols), 0)
@@ -245,7 +246,11 @@
         hi, lo = split(jnp.concatenate([f[p], f[p + 1]], axis=-1))
         for j in range(2):
             at = slice(cols * j, cols * j + cols)
-            part_y[p + j] = dot(jnp.concatenate([hi[:, at], lo[:, at]], axis=-1), wy[...])
+            if p < ahead:
+                weights = jnp.concatenate([wy[...], wy_more[:cols]], axis=0)
+                part_y[p + j] = dot(jnp.concatenate([hi[:, at], lo[:, at], hi[:, at]], axis=-1), weights)
+            else:
+                part_y[p + j] = dot(jnp.concatenate([hi[:, at], lo[:, at]], axis=-1), wy[...])
         for j, r in enumerate(x_operator(hi, lo, wx, deriv_rim)):
             q = p + j
             dx[q] = r
@@ -259,6 +264,11 @@
             for k in range(4):
                 down[1 + k, row, :] = f[q, k : k + 1, :]
                 up[1 + k, row, :] = f[q, n - 4 + k : n - 3 + k, :]
+
+        if lag <= p < ahead + lag:
+            hi, lo = split(jnp.concatenate([part_y[p - lag, :, cols:], part_y[p - lag + 1, :, cols:]], axis=-1))
+            for j, r in enumerate(x_operator(hi, lo, wx_f, filter_rim)):
+                part_y[p - lag + j, :, cols:] = r
 
     sweep(planes, body, written)
     rows = jnp.concatenate([down[k] for k in range(5)] + [up[k] for k in range(5)], axis=0)
@@ -283,13 +293,21 @@
     up[6] = x_up[4]
 
 
-def late_kernel(f, part_y, lower, upper, wy, wx, dy_out, sm_out, sm_low, sm_high, halo, dy, gy, sm, sems):
+def late_kernel(f, part_y, lower, upper, wy, wx, wy_ahead, ax, dy_out, sm_out, sm_low, sm_high, halo, dy, gy, sm, sems):
     planes, n, cols = f.shape
+    rows = jnp.concatenate([h[k, :ahead, :] for h in (lower, upper) for k in range(5)], axis=0)
+    done = dot3(rows, ax[...])
+    table = []
+    for h, first in ((lower, 0), (upper, 5)):
+        for k in range(5):
+            at = (first + k) * ahead
+            table.append(jnp.concatenate([done[at : at + ahead], h[k, ahead:, :]], axis=0))
+        table.append(h[5])
+    table += [lower[4], upper[1]]
     zero = jnp.zeros((planes, 128), F32)
     for c in range(0, n, 128):
         for k in range(16):
-            rows = lower[k, :, c : c + 128] if k < 6 else upper[k - 6, :, c : c + 128] if k < 12 else zero
-            halo[c // 128, pl.ds(k, planes, stride=16), :] = rows
+            halo[c // 128, pl.ds(k, planes, stride=16), :] = table[k][:, c : c + 128] if k < len(table) else zero
     inner = pl.ds(filter_rim, n - 2 * filter_rim)
 
     started = []
@@ -298,33 +316,47 @@
         started.append(pltpu.make_async_copy(source, target, number))
         started[-1].start()
 
+    def faces(q):
+        at = slice(16 * q, 16 * q + 16)
+        hi, lo = split(jnp.concatenate([halo[c, at, :] for c in range(n // 128)], axis=-1))
+        return jnp.concatenate([hi, lo, hi], axis=0).T
+
+    def keep(q, r):
+        sm[q] = r
+        sm_low[q] = r[:filter_rim]
+        sm_high[q] = r[n - filter_rim :]
+
     def y_rows(p):
         for q in (p, p + 1):
-            at = slice(16 * q, 16 * q + 16)
-            hi, lo = split(jnp.concatenate([halo[c, at, :] for c in range(n // 128)], axis=-1))
-            faces = jnp.concatenate([hi, lo, hi], axis=0).T
-            r = dot(jnp.concatenate([f[q].astype(BF16), faces], axis=-1), wy[...]) + part_y[q]
+            if q < ahead:
+                r = dot(faces(q), wy_ahead[...]) + part_y[q]
+                keep(q, r[:, cols:])
+            else:
+                r = dot(jnp.concatenate([f[q].astype(BF16), faces(q)], axis=-1), wy[...]) + part_y[q]
+                gy[q] = r[:, cols:]
             dy[q] = r[:, :cols]
-            gy[q] = r[:, cols:]
 
     def x_rows(p):
         hi, lo = split(jnp.concatenate([gy[p], gy[p + 1]], axis=-1))
         for j, r in enumerate(x_operator(hi, lo, wx, filter_rim)):
-            sm[p + j] = r
-            sm_low[p + j] = r[:filter_rim]
-            sm_high[p + j] = r[n - filter_rim :]
+            keep(p + j, r)
+
+    def send_filtered(p):
+        if (p + 2) % chunk == 0:
+            part = pl.ds(p + 2 - chunk, chunk)
+            send(sm.at[part, inner], sm_out.at[part, inner], sems.at[1, p // chunk])
 
     for p in range(0, planes + lag, 2):
         if p < planes:
             y_rows(p)
-        if p >= lag:
+            if (p + 2) % chunk == 0:
+                part = pl.ds(p + 2 - chunk, chunk)
+                send(dy.at[part], dy_out.at[part], sems.at[0, p // chunk])
+            if p < ahead:
+                send_filtered(p)
+        if p >= ahead + lag:
             x_rows(p - lag)
-        if p < planes and (p + 2) % chunk == 0:
-            part = pl.ds(p + 2 - chunk, chunk)
-            send(dy.at[part], dy_out.at[part], sems.at[0, p // chunk])
-        if p >= lag and (p - lag + 2) % chunk == 0:
-            part = pl.ds(p - lag + 2 - chunk, chunk)
-            send(sm.at[part, inner], sm_out.at[part, inner], sems.at[1, (p - lag) // chunk])
+            send_filtered(p - lag)
     for copy in started:
         copy.wait()
 
@@ -377,6 +409,12 @@
     v[5, :cols], v[4, :cols] = low[:, 0], low[:, 4]
     v[11, :cols], v[7, :cols] = high[:, 0], high[:, 1]
     v_hi, v_lo = halves(v)
+    ahead_v = v.copy()
+    ahead_v[[4, 7], :cols] = 0.0
+    ahead_v[[12, 13], :cols] = v[[4, 7], :cols]
+    ahead_hi, ahead_lo = halves(ahead_v)
+    t["wy_ahead"] = np.concatenate([ahead_hi, ahead_hi, ahead_lo], axis=0)
+    t["ax"] = np.concatenate(halves(smooth.block(rows).T), axis=1)
     t["wy"] = np.concatenate([hi, hi], axis=0)
     t["wy_more"] = np.concatenate([lo, v_hi, v_hi, v_lo], axis=0)
     powers = lambda line, count: line.ratio ** np.arange(count)
@@ -432,7 +470,7 @@
     dx, part_y, dx_low, dx_high, x_down, x_up, own = call(
         "local", local_kernel,
         [block, (planes, rows, 2 * cols), dx_rim, dx_rim, (6, planes, cols), (6, planes, cols), (10 * planes, cols)],
-        [f, t["wx_d"], t["wy"], t["by"]], 4 * 10**9, 10**7,
+        [f] + [t[k] for k in ("wx_d", "wy", "wy_more", "wx_f", "by")], 4 * 10**9, 10**7,
         out_specs=[ANY] + [VMEM] * 6, scratch=[pltpu.VMEM(block, F32), pltpu.SemaphoreType.DMA((copies,))],
     )
     x_down, x_up = call(
@@ -442,7 +480,7 @@
     x_upper = shifted(x_down, "gx", -1)
     dy, sm, sm_low, sm_high = call(
         "late", late_kernel, [block, block, sm_rim, sm_rim],
-        [f, part_y, y_lower, y_upper, t["wy_more"], t["wx_f"]], 6 * 10**9, 2 * 10**7,
+        [f, part_y, y_lower, y_upper] + [t[k] for k in ("wy_more", "wx_f", "wy_ahead", "ax")], 6 * 10**9, 2 * 10**7,
         out_specs=[ANY, ANY, VMEM, VMEM],
         scratch=[
             pltpu.VMEM((rows // 128, planes * 16, 128), F32),

time: 26.7 us -> 26.5 us (level)
  waiting for transfers between devices: 1.71 us -> 0.42 us
  Pallas kernels: 14.5 us -> 15.5 us
    ppermute x4, waiting for transfers between devices: 1.71 us -> 0.42 us  [shifted(): lax.ppermute(values, axis, [(i, (i + by) % count) for i in range(count)])]
    pallas_call x5, Pallas kernels: 14.5 us -> 15.5 us  [call(): pl.pallas_call(kernel, in_specs=in_specs or [VMEM] * len(ins), out_specs=...]
  transfers between devices with their start and end apart: 4 -> 4, of which waited for: 1 -> 1; matrix products, arithmetic and copies ran while one was open for 0% -> 0% of each run, Pallas kernels for 33% -> 37%
where the time goes in v5:
time: 26.5 us; the launch traced here: 26.4 us
  Pallas kernels  15.5 us (58%)
  starting transfers between devices  9.43 us (36%)
  between operations  0.89 us (3%)
  waiting for transfers between devices  0.42 us (2%)
    pallas_call x5, Pallas kernels, call(): pl.pallas_call(kernel, in_specs=in_specs or [VMEM] * len(ins), out_specs=...  15.5 us
    ppermute x4, starting transfers between devices, shifted(): lax.ppermute(values, axis, [(i, (i + by) % count) for i in range(count)])  9.43 us
  transfers between devices with their start and end apart: 4, of which 1 were waited for; matrix products, arithmetic and copies ran while one was open for 0% of the time, Pallas kernels for 37%

profile of v5, /device:TPU:0, one launch (start us, length us, event | category | flops | bytes accessed | tf_op | source)
XLA Modules:
  0.0 26.4 jit_solution(12339397673051164075)
XLA Ops:
  0.6 0.0 copy-start.14
  0.6 0.0 copy-start.10
  0.7 0.0 copy-start.15
  0.7 0.0 copy-start.13
  0.7 0.0 copy-start.12
  0.7 3.5 %faces.1 = (f32[40,256,128]{2,1,0:T(8,128)S(1)}, f32[6,40,256]{2,1,0:T(8,128)S(1)}, f32[6,40,256]{2,1,0:T(8,128)S(1)}) custom-call(f32[40,256,128]{2,1,0:T(8,128)} %bitcast.6), custom_call_target="tpu_custom_call" | custom-call | flops 1000000000 | bytes 10000000 | tf_op jit(solution)/shard_map/faces/pallas_call | solution.py:119
  4.2 1.6 %collective-permute-start = (f32[6,40,256]{2,1,0:T(8,128)S(1)}, f32[6,40,256]{2,1,0:T(8,128)S(1)}, u32[]{:S(2)}, u32[]{:S(2)}) collective-permute-start(f32[6,40,256]{2,1,0:T(8,128)S(1)} %get-tuple-element.25), channel_id=1, source_target_pairs={{0,1},{1,2},{2,3},{3,4},{4,5},{5,6},{6,7},{7,8},{8,9},{9,10},{10,1... | collective-permute-start | bytes 737288 | tf_op jit(solution)/shard_map/ppermute | solution.py:450
  5.8 4.8 %collective-permute-start.1 = (f32[6,40,256]{2,1,0:T(8,128)S(1)}, f32[6,40,256]{2,1,0:T(8,128)S(1)}, u32[]{:S(2)}, u32[]{:S(2)}) collective-permute-start(f32[6,40,256]{2,1,0:T(8,128)S(1)} %get-tuple-element.26), channel_id=1, source_target_pairs={{0,15},{1,0},{2,1},{3,2},{4,3},{5,4},{6,5},{7,6},{8,7},{9,8},{10,9... | collective-permute-start | bytes 737288 | tf_op jit(solution)/shard_map/ppermute | solution.py:450
  10.7 0.0 copy-start
  10.7 0.0 copy-start.1
  10.7 0.0 copy-start.11
  10.7 0.0 copy-start.16
  10.7 5.4 %local.1 = (f32[40,256,128]{2,1,0:T(8,128)}, f32[40,256,256]{2,1,0:T(8,128)S(1)}, f32[40,24,128]{2,1,0:T(8,128)S(1)}, f32[40,24,128]{2,1,0:T(8,128)S(1)}, f32[6,...) custom-call(f32[40,256,128]{2,1,0:T(8,128)S(1)} %get-tuple-element.21.f, ...), custom_call_target="tpu_custom_call" | custom-call | flops 4000000000 | bytes 10000000 | tf_op jit(solution)/shard_map/local/pallas_call | solution.py:119
  16.1 0.4 %collective-permute-done.lower = f32[6,40,256]{2,1,0:T(8,128)S(1)} collective-permute-done((f32[6,40,256]{2,1,0:T(8,128)S(1)}, f32[6,40,256]{2,1,0:T(8,128)S(1)}, u32[]{:S(2)}, u32[]{:S(2)}) %collective-permute-start) | collective-permute-done | bytes 245792 | tf_op jit(solution)/shard_map/ppermute | solution.py:450
  16.5 0.6 %x_faces.1 = (f32[7,40,128]{2,1,0:T(8,128)S(1)}, f32[7,40,128]{2,1,0:T(8,128)S(1)}) custom-call(f32[400,128]{1,0:T(8,128)S(1)} %get-tuple-element.29.own, f32[6,40,128]{2,1,0:T(8,128)S(1)} %get-tuple-element.30.x_down, f32[6,40,128]{2,1,0:T(8,128)S(1)} %get-tuple-element.31.x_up, f32[6,40,256]{2,1,0:T(8,128)S(1)} %collective-permute-done.lower, ...), custom_call_target="tpu_custom_call" | custom-call | flops 100000000 | bytes 1000000 | tf_op jit(solution)/shard_map/x_faces/pallas_call | solution.py:119
  17.2 0.0 collective-permute-start.2
  17.2 2.9 %collective-permute-start.3 = (f32[7,40,128]{2,1,0:T(8,128)S(1)}, f32[7,40,128]{2,1,0:T(8,128)S(1)}, u32[]{:S(2)}, u32[]{:S(2)}) collective-permute-start(f32[7,40,128]{2,1,0:T(8,128)S(1)} %get-tuple-element.33), channel_id=1, source_target_pairs={{0,112},{16,0},{32,16},{48,32},{64,48},{80,64},{96,80},{112,96},{1... | collective-permute-start | bytes 430088 | tf_op jit(solution)/shard_map/ppermute | solution.py:450
  20.2 0.0 copy-start.4
  20.2 0.0 copy-start.5
  20.2 0.0 copy-start.7
  20.2 0.0 copy-start.8
  20.2 0.0 copy-start.9
  20.3 4.3 %late.1 = (f32[40,256,128]{2,1,0:T(8,128)}, f32[40,256,128]{2,1,0:T(8,128)}, f32[40,40,128]{2,1,0:T(8,128)S(1)}, f32[40,40,128]{2,1,0:T(8,128)S(1)}) custom-call(f32[40,256,128]{2,1,0:T(8,128)S(1)} %get-tuple-element.21.f, f32[40,256,256]{2,1,0:T(8,128)S(1)} %get-tuple-element.24.part_y, f32[6,40,256]{2,1,0:T(8,128)S(1)} %collective-permute-done.lower, ...), custom_call_target="tpu_custom_call" | custom-call | flops 6000000000 | bytes 20000000 | tf_op jit(solution)/shard_map/late/pallas_call | solution.py:119
  24.7 1.7 %rims.1 = (f32[40,256,128]{2,1,0:T(8,128)}, f32[40,256,128]{2,1,0:T(8,128)}) custom-call(f32[40,24,128]{2,1,0:T(8,128)S(1)} %get-tuple-element.22.dx_low, f32[40,24,128]{2,1,0:T(8,128)S(1)} %get-tuple-element.23.dx_high, f32[40,40,128]{2,1,0:T(8,128)S(1)} %get-tuple-element.27.sm_low, ...), custom_call_target="tpu_custom_call", output_to_operand_aliasing={{0}: (14, {}), {1}: (15, {})} | custom-call | flops 100000000 | bytes 4000000 | tf_op jit(solution)/shard_map/rims/pallas_call | solution.py:119
  (23 shorter events, 0.1 us)
Async XLA Ops:
  0.6 10.0 %copy-start.14 = (bf16[176,256]{1,0:T(8,128)(2,1)S(1)}, bf16[176,256]{1,0:T(8,128)(2,1)}, u32[]{:S(2)}) copy-start(bf16[176,256]{1,0:T(8,128)(2,1)} %constant.39.clone.wy_more.wy) | copy-start | bytes 270340
  0.6 10.0 %copy-start.10 = (bf16[512,256]{1,0:T(8,128)(2,1)S(1)}, bf16[512,256]{1,0:T(8,128)(2,1)}, u32[]{:S(2)}) copy-start(bf16[512,256]{1,0:T(8,128)(2,1)} %constant.35.clone.wx_f.wx) | copy-start | bytes 786436
  0.7 10.0 %copy-start.15 = (bf16[128,256]{1,0:T(8,128)(2,1)S(1)}, bf16[128,256]{1,0:T(8,128)(2,1)}, u32[]{:S(2)}) copy-start(bf16[128,256]{1,0:T(8,128)(2,1)} %constant.40.clone.by) | copy-start | bytes 196612
  0.7 10.0 %copy-start.13 = (bf16[256,256]{1,0:T(8,128)(2,1)S(1)}, bf16[256,256]{1,0:T(8,128)(2,1)}, u32[]{:S(2)}) copy-start(bf16[256,256]{1,0:T(8,128)(2,1)} %constant.38.clone.wy) | copy-start | bytes 393220
  0.7 10.0 %copy-start.12 = (bf16[512,256]{1,0:T(8,128)(2,1)S(1)}, bf16[512,256]{1,0:T(8,128)(2,1)}, u32[]{:S(2)}) copy-start(bf16[512,256]{1,0:T(8,128)(2,1)} %constant.34.clone.wx) | copy-start | bytes 786436
  4.2 12.3 %collective-permute-start = (f32[6,40,256]{2,1,0:T(8,128)S(1)}, f32[6,40,256]{2,1,0:T(8,128)S(1)}, u32[]{:S(2)}, u32[]{:S(2)}) collective-permute-start(f32[6,40,256]{2,1,0:T(8,128)S(1)} %get-tuple-element.25), channel_id=1, source_target_pairs={{0,1},{1,2},{2,3},{3,4},{4,5},{5,6},{6,7},{7,8},{8,9},{9,10},{10,1... | collective-permute-start | bytes 737288 | tf_op jit(solution)/shard_map/ppermute | solution.py:450
  5.8 10.7 %collective-permute-start.1 = (f32[6,40,256]{2,1,0:T(8,128)S(1)}, f32[6,40,256]{2,1,0:T(8,128)S(1)}, u32[]{:S(2)}, u32[]{:S(2)}) collective-permute-start(f32[6,40,256]{2,1,0:T(8,128)S(1)} %get-tuple-element.26), channel_id=1, source_target_pairs={{0,15},{1,0},{2,1},{3,2},{4,3},{5,4},{6,5},{7,6},{8,7},{9,8},{10,9... | collective-permute-start | bytes 737288 | tf_op jit(solution)/shard_map/ppermute | solution.py:450
  10.7 5.9 %copy-start = (bf16[256,256]{1,0:T(8,128)(2,1)S(1)}, bf16[256,256]{1,0:T(8,128)(2,1)}, u32[]{:S(2)}) copy-start(bf16[256,256]{1,0:T(8,128)(2,1)} %constant.41.clone.tx) | copy-start | bytes 393220
  10.7 5.8 %copy-start.1 = (bf16[128,256]{1,0:T(8,128)(2,1)S(1)}, bf16[128,256]{1,0:T(8,128)(2,1)}, u32[]{:S(2)}) copy-start(bf16[128,256]{1,0:T(8,128)(2,1)} %constant.42.clone.vy) | copy-start | bytes 196612
  10.7 9.5 %copy-start.11 = (bf16[256,512]{1,0:T(8,128)(2,1)S(1)}, bf16[256,512]{1,0:T(8,128)(2,1)}, u32[]{:S(2)}) copy-start(bf16[256,512]{1,0:T(8,128)(2,1)} %constant.37.clone.ax) | copy-start | bytes 786436
  10.7 9.5 %copy-start.16 = (bf16[48,256]{1,0:T(8,128)(2,1)S(1)}, bf16[48,256]{1,0:T(8,128)(2,1)}, u32[]{:S(2)}) copy-start(bf16[48,256]{1,0:T(8,128)(2,1)} %constant.36.clone.wy_ahead) | copy-start | bytes 73732
  17.2 7.4 %collective-permute-start.2 = (f32[7,40,128]{2,1,0:T(8,128)S(1)}, f32[7,40,128]{2,1,0:T(8,128)S(1)}, u32[]{:S(2)}, u32[]{:S(2)}) collective-permute-start(f32[7,40,128]{2,1,0:T(8,128)S(1)} %get-tuple-element.32), channel_id=1, source_target_pairs={{0,16},{16,32},{32,48},{48,64},{64,80},{80,96},{96,112},{112,0},{1... | collective-permute-start | bytes 430088 | tf_op jit(solution)/shard_map/ppermute | solution.py:450
  17.2 7.4 %collective-permute-start.3 = (f32[7,40,128]{2,1,0:T(8,128)S(1)}, f32[7,40,128]{2,1,0:T(8,128)S(1)}, u32[]{:S(2)}, u32[]{:S(2)}) collective-permute-start(f32[7,40,128]{2,1,0:T(8,128)S(1)} %get-tuple-element.33), channel_id=1, source_target_pairs={{0,112},{16,0},{32,16},{48,32},{64,48},{80,64},{96,80},{112,96},{1... | collective-permute-start | bytes 430088 | tf_op jit(solution)/shard_map/ppermute | solution.py:450
  20.2 4.4 %copy-start.2 = (f32[40,128]{1,0:T(8,128)S(1)}, f32[40,128]{1,0:T(8,128)}, u32[]{:S(2)}) copy-start(f32[40,128]{1,0:T(8,128)} %constant.44.clone.fs_high) | copy-start | bytes 61444
  20.2 4.4 %copy-start.3 = (f32[40,128]{1,0:T(8,128)S(1)}, f32[40,128]{1,0:T(8,128)}, u32[]{:S(2)}) copy-start(f32[40,128]{1,0:T(8,128)} %constant.43.clone.fs_low) | copy-start | bytes 61444
  20.2 4.4 %copy-start.4 = (f32[4,8,128]{2,1,0:T(8,128)S(1)}, f32[4,8,128]{2,1,0:T(8,128)}, u32[]{:S(2)}) copy-start(f32[4,8,128]{2,1,0:T(8,128)} %constant.46.clone.fc_high) | copy-start | bytes 49156
  20.2 4.4 %copy-start.5 = (f32[4,8,128]{2,1,0:T(8,128)S(1)}, f32[4,8,128]{2,1,0:T(8,128)}, u32[]{:S(2)}) copy-start(f32[4,8,128]{2,1,0:T(8,128)} %constant.45.clone.fc_low) | copy-start | bytes 49156
  20.2 4.4 %copy-start.6 = (f32[24,128]{1,0:T(8,128)S(1)}, f32[24,128]{1,0:T(8,128)}, u32[]{:S(2)}) copy-start(f32[24,128]{1,0:T(8,128)} %constant.48.clone.ds_high) | copy-start | bytes 36868
  20.2 4.4 %copy-start.7 = (f32[24,128]{1,0:T(8,128)S(1)}, f32[24,128]{1,0:T(8,128)}, u32[]{:S(2)}) copy-start(f32[24,128]{1,0:T(8,128)} %constant.47.clone.ds_low) | copy-start | bytes 36868
  20.2 4.4 %copy-start.8 = (f32[8,128]{1,0:T(8,128)S(1)}, f32[8,128]{1,0:T(8,128)}, u32[]{:S(2)}) copy-start(f32[8,128]{1,0:T(8,128)} %constant.50.clone.dc_high) | copy-start | bytes 12292
  20.2 4.4 %copy-start.9 = (f32[8,128]{1,0:T(8,128)S(1)}, f32[8,128]{1,0:T(8,128)}, u32[]{:S(2)}) copy-start(f32[8,128]{1,0:T(8,128)} %constant.49.clone.dc_low) | copy-start | bytes 12292
